TPU v7x, 512 devices: a whole 4x4x16 slice. The times are simulated.
512 devices in a mesh: pair: 64 (over x, z), tensor: 8 (over y, core).
Axes of the slice: x: 4, y: 4, z: 16, core: 2. Of those that a mesh axis runs over, the one named last changes fastest.
Arguments:
- rollout: bfloat16 [6144, 4608], P('pair', 'tensor'), may hold values from -6 to 6
- counts: int32 [64, 64], P('pair'), may hold values from 0 to 3, as said below
- lengths: int32 [192], replicated, may hold values from 1 to 32, 3840 in all
- partner_slot: int32 [64, 3], P('pair'), may hold values from 0 to 2, as said below
- pre_gain: float32 [4608], replicated, may hold values from 0.5 to 6
- post_gain: float32 [4608], P('tensor'), may hold values from 0.1 to 1.9
- query_weight: bfloat16 [4608, 2048], P('pair', 'tensor'), may hold values from -0.09375 to 0.09375
- key_weight: bfloat16 [4608, 1024], P('pair', 'tensor'), may hold values from -0.09375 to 0.09375
- value_weight: bfloat16 [4608, 1024], P('pair', 'tensor'), may hold values from -0.09375 to 0.09375
- out_weight: bfloat16 [4608, 2048], P('pair', 'tensor'), may hold values from -0.125 to 0.125
Outputs:
- layer_out: bfloat16 [6144, 4608], P('pair', 'tensor')
Inputs may be any that keep to these rules, and one draw needn't show every extreme that they name: `counts`: every source shard sends 96 rows in all and every judge shard receives 96 rows in all. The matching pairs shard d with the shard half the pair axis away; partner_slot on the two shards are inverse permutations, so the partner of a partner is the response itself.
All inputs are finite; a program needn't handle non-finite values.
Results may differ from a plain program's by a relative error of at most 0.013.
Values may be sent and summed in bfloat16 or wider, within the bound.
A program may use at most 64 MiB of HBM per device.

v0:
```python
import jax
import jax.numpy as jnp
from jax import lax
from jax.sharding import PartitionSpec as P

HD = 128
LEN = 32


score_scale = 144.0 ** (-0.5)
soft_cap = 50.0
epsilon = 1e-06
negative = -1e30


def from_behind(x, axis, by):
    length = lax.axis_size(axis)
    return lax.ppermute(x, axis, [(i, (i + by) % length) for i in range(length)])


def attend(queries, key_rows, values, partner_keys, partner_values, own_len, far_len):
    responses, length_rows = (queries.shape[0], queries.shape[1])
    keys_all = jnp.concatenate((key_rows, partner_keys), axis=1)
    values_all = jnp.concatenate((values, partner_values), axis=1)
    scores = (
        jnp.einsum("rqkgd,rskd->rkgqs", queries, keys_all, preferred_element_type=jnp.float32)
        * score_scale
    )
    scores = soft_cap * jnp.tanh(scores / soft_cap)
    key_spot = jnp.arange(2 * length_rows, dtype=jnp.int32)
    query_spot = jnp.arange(length_rows, dtype=jnp.int32)
    own_ok = (key_spot[None, None, :] <= query_spot[None, :, None]) & (
        key_spot[None, None, :] < own_len[:, None, None]
    )
    far_ok = (key_spot[None, None, :] >= length_rows) & (
        key_spot[None, None, :] - length_rows < far_len[:, None, None]
    )
    allowed = own_ok | far_ok
    scores = jnp.where(allowed[:, None, None, :, :], scores, negative)
    powers = jnp.exp(scores)
    probs = (powers / jnp.sum(powers, axis=-1, keepdims=True)).astype(jnp.bfloat16)
    context = jnp.einsum("rkgqs,rskd->rqkgd", probs, values_all, preferred_element_type=jnp.float32)
    filled = query_spot[None, :] < own_len[:, None]
    context = jnp.where(filled[:, :, None, None, None], context, 0.0)
    return context.astype(jnp.bfloat16).reshape(responses * length_rows, -1)


def shards(
    rollout,
    counts,
    lengths,
    partner_slot,
    pre_gain,
    post_gain,
    query_weight,
    key_weight,
    value_weight,
    out_weight,
):
    pair_count = lax.axis_size("pair")
    row_count, slice_width = rollout.shape
    capacity = 2 * row_count // pair_count
    sending = counts.reshape(pair_count)
    starts = jnp.cumsum(sending) - sending
    slot_ids = jnp.arange(capacity, dtype=jnp.int32)
    picked = (starts[:, None] + slot_ids[None, :]).reshape(-1)
    filled = (slot_ids[None, :] < sending[:, None]).reshape(-1)
    bucket = jnp.take(rollout, jnp.minimum(picked, row_count - 1), axis=0)
    bucket = jnp.where(filled[:, None], bucket, jnp.zeros((), rollout.dtype)).reshape(
        pair_count, capacity, slice_width
    )
    arrived, arrived_counts = (
        lax.all_to_all(bucket, "pair", split_axis=0, concat_axis=0, tiled=True),
        lax.all_to_all(
            sending.reshape(pair_count, 1), "pair", split_axis=0, concat_axis=0, tiled=True
        ),
    )
    arrived_counts = arrived_counts.reshape(pair_count)
    through = jnp.cumsum(arrived_counts)
    before = through - arrived_counts
    row_ids = jnp.arange(row_count, dtype=jnp.int32)
    source = jnp.sum((through[:, None] <= row_ids[None, :]).astype(jnp.int32), axis=0)
    is_source = jnp.arange(pair_count, dtype=jnp.int32)[:, None] == source[None, :]
    begins = jnp.sum(jnp.where(is_source, before[:, None], 0), axis=0)
    relaid = jnp.take(
        arrived.reshape(pair_count * capacity, slice_width),
        source * capacity + row_ids - begins,
        axis=0,
    )
    wide_rows = lax.all_gather(relaid, "tensor", axis=1, tiled=True)
    x_wide = wide_rows.astype(jnp.float32)
    normed = (
        x_wide * lax.rsqrt(jnp.mean(x_wide * x_wide, axis=1, keepdims=True) + epsilon) * pre_gain
    ).astype(jnp.bfloat16)
    full_query, full_key, full_value, full_out = (
        lax.all_gather(query_weight, "pair", axis=0, tiled=True),
        lax.all_gather(key_weight, "pair", axis=0, tiled=True),
        lax.all_gather(value_weight, "pair", axis=0, tiled=True),
        lax.all_gather(out_weight, "pair", axis=0, tiled=True),
    )
    queries = jnp.dot(normed, full_query, preferred_element_type=jnp.float32)
    key_rows = jnp.dot(normed, full_key, preferred_element_type=jnp.float32)
    values = jnp.dot(normed, full_value, preferred_element_type=jnp.float32)
    head_count = query_weight.shape[1] // HD
    kv_count = key_weight.shape[1] // HD
    grouped = head_count // kv_count
    responses = row_count // LEN
    queries = queries.astype(jnp.bfloat16).reshape(responses, LEN, kv_count, grouped, HD)
    key_rows = key_rows.astype(jnp.bfloat16).reshape(responses, LEN, kv_count, HD)
    values = values.astype(jnp.bfloat16).reshape(responses, LEN, kv_count, HD)
    partner_kv = from_behind(jnp.stack((key_rows, values)), "pair", pair_count // 2)
    slot_row = partner_slot.reshape(responses)
    partner_kv = jnp.take(partner_kv, slot_row, axis=1)
    my_pair = lax.axis_index("pair")
    facing_pair = (my_pair + pair_count // 2) % pair_count
    own_len = lax.dynamic_slice_in_dim(lengths, my_pair * responses, responses)
    far_len = jnp.take(
        lax.dynamic_slice_in_dim(lengths, facing_pair * responses, responses), slot_row
    )
    context = attend(queries, key_rows, values, partner_kv[0], partner_kv[1], own_len, far_len)
    partial_sum = lax.dot_general(
        context, full_out, (((1,), (1,)), ((), ())), preferred_element_type=jnp.float32
    )
    attended = lax.psum(partial_sum.astype(jnp.bfloat16), "tensor").astype(jnp.float32)
    mean_square = jnp.mean(attended * attended, axis=1)
    my_share = lax.dynamic_slice_in_dim(
        attended, lax.axis_index("tensor") * slice_width, slice_width, 1
    )
    scale_rows = lax.rsqrt(mean_square + epsilon)[:, None]
    return (relaid.astype(jnp.float32) + my_share * scale_rows * post_gain).astype(jnp.bfloat16)


def solution(mesh):
    placed = (
        P("pair", "tensor"),
        P("pair", None),
        P(),
        P("pair", None),
        P(),
        P("tensor"),
        P("pair", "tensor"),
        P("pair", "tensor"),
        P("pair", "tensor"),
        P("pair", "tensor"),
    )
    return jax.shard_map(
        shards, mesh=mesh, in_specs=placed, out_specs=P("pair", "tensor"), check_vma=False
    )
```

profile of v0, /device:TPU:1, one launch (start us, length us, event | category | flops | bytes accessed | tf_op | source)
XLA Modules:
  0.0 660.6 jit_solution(17939083348202923245)
XLA Ops:
  6.5 0.7 all-gather.8.cloned.1.call-update
  7.3 0.7 all-gather.6.cloned.1.call-update
  8.1 0.7 all-gather.10.cloned.1.call-update
  8.7 1.4 copy.49
  10.1 19.1 %all-to-all-start = ((s32[64,1,1]{2,1,0:T(1,128)}), s32[64,1,1]{2,1,0:T(1,128)S(1)}, u32[]{:S(2)}, u32[]{:S(2)}) async-start(s32[64,1,1]{2,1,0:T(1,128)} %copy.49), calls=%async_computation | async-start | bytes 65536 | tf_op jit(solution)/shard_map/all_to_all | solution.py:74
  29.3 0.5 all-gather.12.cloned.1.call-update
  29.8 0.7 copy.51
  30.7 0.1 reduce.4
  30.8 0.7 bitcast_subtract_fusion.1
  31.5 0.7 fusion.18
  32.2 0.8 fusion.21
  33.0 0.6 gather_fusion.3
  33.6 0.7 broadcast_select_fusion.1
  34.4 0.1 min.21
  34.6 1.0 gather_fusion
  35.6 0.1 gather.19
  35.7 0.1 copy.52
  35.9 1.1 select_select_fusion
  37.1 5.3 all-to-all-done
  42.4 9.2 %all-to-all-start.1 = ((bf16[64,3,576]{2,1,0:T(4,128)(2,1)}), bf16[64,3,576]{2,1,0:T(4,128)(2,1)S(1)}, u32[]{:S(2)}, u32[]{:S(2)}) async-start(bf16[64,3,576]{2,1,0:T(4,128)(2,1)} %select_select_fusion), calls=%async_computation.1 | async-start | bytes 655360 | tf_op jit(solution)/shard_map/all_to_all | solution.py:73
  51.9 0.1 reduce.2
  52.0 1.2 reduce.3
  53.4 19.8 %all-to-all-done.1 = bf16[64,3,576]{2,1,0:T(4,128)(2,1)S(1)} async-done(((bf16[64,3,576]{2,1,0:T(4,128)(2,1)}), bf16[64,3,576]{2,1,0:T(4,128)(2,1)S(1)}, u32[]{:S(2)}, u32[]{:S(2)}) %all-to-all-start.1) | async-done | bytes 221216 | tf_op jit(solution)/shard_map/all_to_all | solution.py:73
  73.2 0.2 reshape.406
  73.4 0.8 gather_fusion.1
  74.3 17.5 %all-gather = bf16[8,576,96]{1,2,0:T(8,128)(2,1)S(1)} all-gather(bf16[1,576,96]{1,2,0:T(8,128)(2,1)S(1)} %fusion.8), channel_id=1, replica_groups=mesh['pair'=64,'tensor'=8] {'tensor'}, dimensions={0}, use_global_device_ids=true | all-gather | bytes 995328 | tf_op jit(solution)/shard_map/all_gather | solution.py:90
  91.8 1.6 copy.54
  93.4 1.7 reshape.452
  95.2 0.2 multiply_reduce_fusion
  95.4 0.5 copy-done.1
  95.9 0.2 multiply_convert_fusion
  96.2 50.7 %all-gather.8.cloned.1.call-done = bf16[4608,128]{1,0:T(8,128)(2,1)} async-done(((bf16[72,128]{1,0:T(8,128)(2,1)}), bf16[4608,128]{1,0:T(8,128)(2,1)}) %all-gather.8.cloned.1.call-update) | async-done | bytes 1179664 | tf_op jit(solution)/shard_map/all_gather | solution.py:97
  146.9 1.7 convolution_convert_fusion.2
  148.6 136.5 %all-gather.6.cloned.1.call-done = bf16[4608,128]{1,0:T(8,128)(2,1)} async-done(((bf16[72,128]{1,0:T(8,128)(2,1)}), bf16[4608,128]{1,0:T(8,128)(2,1)}) %all-gather.6.cloned.1.call-update) | async-done | bytes 1179664 | tf_op jit(solution)/shard_map/all_gather | solution.py:98
  285.1 1.7 convolution_convert_fusion.3
  286.8 3.9 collective-permute-start
  290.8 2.4 collective-permute-done
  293.1 0.6 gather_fusion.2
  293.8 132.8 %all-gather.10.cloned.1.call-done = bf16[4608,256]{1,0:T(8,128)(2,1)} async-done(((bf16[72,256]{1,0:T(8,128)(2,1)}), bf16[4608,256]{1,0:T(8,128)(2,1)}) %all-gather.10.cloned.1.call-update) | async-done | bytes 2359312 | tf_op jit(solution)/shard_map/all_gather | solution.py:96
  426.6 2.2 convolution_convert_fusion.1
  428.8 0.3 fusion.22
  429.0 0.2 fusion.7
  429.3 137.3 %all-gather.12.cloned.1.call-done = bf16[4608,256]{1,0:T(8,128)(2,1)} async-done(((bf16[72,256]{1,0:T(8,128)(2,1)}), bf16[4608,256]{1,0:T(8,128)(2,1)}) %all-gather.12.cloned.1.call-update) | async-done | bytes 2359312 | tf_op jit(solution)/shard_map/all_gather | solution.py:99
  566.6 3.4 convolution_convert_fusion
  570.1 80.3 %all-reduce.2.cloned.1.call-done = bf16[96,4608]{1,0:T(8,128)(2,1)} async-done(((bf16[96,4608]{1,0:T(8,128)(2,1)}), bf16[96,4608]{1,0:T(8,128)(2,1)}) %all-reduce.2.cloned.1.call-update) | async-done | bytes 884752 | tf_op jit(solution)/shard_map/psum | solution.py:124
  650.4 1.4 multiply_reduce_fusion.1
  651.9 1.3 convert_element_type.50
  653.2 0.8 add_convert_fusion
  (42 shorter events, 1.2 us)
Async XLA Ops:
  6.5 28.0 %copy-start = (bf16[96,576]{1,0:T(8,128)(2,1)S(1)}, bf16[96,576]{1,0:T(8,128)(2,1)}, u32[]{:S(2)}) copy-start(bf16[96,576]{1,0:T(8,128)(2,1)} %param.10) | copy-start | bytes 331780
  6.5 140.4 %all-gather.8.cloned.1.call-start = ((), (), s32[]{:S(2)}) async-start(), calls=%async_computation.3 | async-start | bytes 1198080 | tf_op jit(solution)/shard_map/all_gather | solution.py:97
  7.3 277.9 %all-gather.6.cloned.1.call-start = ((), (), s32[]{:S(2)}) async-start(), calls=%async_computation.2 | async-start | bytes 1198080 | tf_op jit(solution)/shard_map/all_gather | solution.py:98
  8.0 418.6 %all-gather.10.cloned.1.call-start = ((), (), s32[]{:S(2)}) async-start(), calls=%async_computation.4 | async-start | bytes 2396160 | tf_op jit(solution)/shard_map/all_gather | solution.py:96
  10.1 32.3 %all-to-all-start = ((s32[64,1,1]{2,1,0:T(1,128)}), s32[64,1,1]{2,1,0:T(1,128)S(1)}, u32[]{:S(2)}, u32[]{:S(2)}) async-start(s32[64,1,1]{2,1,0:T(1,128)} %copy.49), calls=%async_computation | async-start | bytes 65536 | tf_op jit(solution)/shard_map/all_to_all | solution.py:74
  29.2 537.4 %all-gather.12.cloned.1.call-start = ((), (), s32[]{:S(2)}) async-start(), calls=%async_computation.5 | async-start | bytes 2396160 | tf_op jit(solution)/shard_map/all_gather | solution.py:99
  30.6 5.3 copy-start.2
  42.4 30.8 %all-to-all-start.1 = ((bf16[64,3,576]{2,1,0:T(4,128)(2,1)}), bf16[64,3,576]{2,1,0:T(4,128)(2,1)S(1)}, u32[]{:S(2)}, u32[]{:S(2)}) async-start(bf16[64,3,576]{2,1,0:T(4,128)(2,1)} %select_select_fusion), calls=%async_computation.1 | async-start | bytes 655360 | tf_op jit(solution)/shard_map/all_to_all | solution.py:73
  51.7 598.7 %all-reduce.2.cloned.1.call-start = ((), (), s32[]{:S(2)}) async-start(), calls=%async_computation.6 | async-start | bytes 1769472 | tf_op jit(solution)/shard_map/psum | solution.py:124
  95.2 0.7 copy-start.1
  286.8 6.3 collective-permute-start
  570.1 83.1 %copy-start.3 = (f32[576]{0:T(1024)S(1)}, f32[576]{0:T(1024)}, u32[]{:S(2)}) copy-start(f32[576]{0:T(1024)} %param.15) | copy-start | bytes 6916
Sparse Core Ops, SparseCore 0:
  10.3 136.5 all-gather.7
  149.9 135.2 all-gather.5
  288.1 138.4 all-gather.9
  429.4 137.1 all-gather.11
  570.2 80.1 all-reduce.1
where the time goes:
time: 662 us; the launch traced here: 661 us
  waiting for transfers between devices  568 us (86%)
  starting transfers between devices  32.4 us (5%)
  blocking collectives  17.5 us (3%)
  between operations  13.4 us (2%)
  local copies, waits for them, and re-layouts  10.6 us (2%)
  other arithmetic  9.44 us (1%)
  matrix products  9.41 us (1%)
    all_gather x1, waiting for transfers between devices, shards(): lax.all_gather(out_weight, 'pair', axis=0, tiled=True)  137 us
    all_gather x1, waiting for transfers between devices, shards(): lax.all_gather(value_weight, 'pair', axis=0, tiled=True)  137 us
    all_gather x1, waiting for transfers between devices, shards(): lax.all_gather(query_weight, 'pair', axis=0, tiled=True)  133 us
    psum x1, waiting for transfers between devices, shards(): lax.psum(partial_sum.astype(jnp.bfloat16), 'tensor').astype(jnp.float32)  80.3 us
    all_gather x1, waiting for transfers between devices, shards(): lax.all_gather(key_weight, 'pair', axis=0, tiled=True)  50.7 us
    all_to_all x1, waiting for transfers between devices, shards(): lax.all_to_all(bucket, 'pair', split_axis=0, concat_axis=0, tiled=True)  19.8 us
    all_to_all x1, starting transfers between devices, shards(): lax.all_to_all(sending.reshape(pair_count, 1), 'pair', split_axis=0, conc...  19.1 us
    all_gather x1, blocking collectives, shards(): wide_rows = lax.all_gather(relaid, 'tensor', axis=1, tiled=True)  17.5 us
  transfers between devices with their start and end apart: 8, of which 8 were waited for; matrix products, arithmetic and copies ran while one was open for 3% of the time, Pallas kernels for 0%

commit v1 on v0

v1 whole, which is shorter than its diff:
```python
import jax
import jax.numpy as jnp
from jax import lax
from jax.experimental import pallas as pl
from jax.experimental.pallas import tpu as pltpu
from jax.sharding import PartitionSpec as P

NX, NY, NZ, NC = 4, 4, 16, 2
NT = NY * NC
HD = 128
LEN = 32
RESP = 3
ROWS = RESP * LEN
FEAT = 576
WIDE = 640
WROWS = 72
BLOCK = NZ * WROWS
CAP = 3
SLOTS = NX * 4
KEPT = NZ * CAP
ALL_SLOTS = NX * KEPT
HALF = ALL_SLOTS // 2

score_scale = 144.0 ** (-0.5)
soft_cap = 50.0
epsilon = 1e-06
negative = -1e30

F32 = jnp.float32
BF16 = jnp.bfloat16
I32 = jnp.int32
MESH = pl.DeviceIdType.MESH
NN = (((1,), (0,)), ((), ()))
NTR = (((1,), (1,)), ((), ()))


def dot(a, b, dims=NN):
    return lax.dot_general(a, b, dims, preferred_element_type=F32)


def iota(shape, dim):
    return lax.broadcasted_iota(I32, shape, dim)


def ones_where(cond):
    return jnp.where(cond, 1.0, 0.0).astype(BF16)


def column_to_row(col):
    rows = col.shape[0]
    same = iota((rows, 128), 0) == iota((rows, 128), 1)
    return jnp.sum(jnp.where(same, col, 0.0), axis=0, keepdims=True)


def row_to_column(row, rows):
    same = iota((rows, 128), 0) == iota((rows, 128), 1)
    return jnp.sum(jnp.where(same, row, 0.0), axis=1, keepdims=True)


def kernel(
    roll, counts, lens, pslot, gain, post, wq, wk, wv, wo, out,
    xin, zsend, zrecv, wsend, wbuf, w32, slot_out, slot_in, xg, xs, judged, sq_in, fin_in,
    part, part_in, far_in, ctx, co_out, co_in, xo_out, xo_in,
    tr_s, tr_r, za_s, za_r, ring_s, ring_r, xg_s, xg_r, cs_s, cs_r, sq_s, sq_r,
    rs_s, rs_r, far_s, far_r, cx_s, cx_r, co_s, co_r, xo_s, xo_r, fn_s, fn_r,
):
    pair = lax.axis_index("pair")
    ten = lax.axis_index("tensor")
    x, z = pair // NZ, pair % NZ
    y, c = ten // NC, ten % NC

    def dev(xx, zz, yy, cc):
        return {"pair": xx * NZ + zz, "tensor": yy * NC + cc}

    def remote(src, dst, send, recv, where):
        return pltpu.make_async_remote_copy(
            src_ref=src, dst_ref=dst, send_sem=send, recv_sem=recv,
            device_id=where, device_id_type=MESH,
        )

    off_diagonal = x != y

    barrier = pltpu.get_barrier_semaphore()

    def greet(where):
        pl.semaphore_signal(barrier, inc=1, device_id=where, device_id_type=MESH)

    @pl.loop(1, NZ)
    def _(k):
        greet(dev(x, (z + k) % NZ, y, c))

    @pl.loop(1, NX)
    def _(k):
        greet(dev((x + k) % NX, z, y, c))

    @pl.loop(1, NT)
    def _(k):
        greet({"pair": pair, "tensor": (ten + k) % NT})

    @pl.when(off_diagonal)
    def _():
        greet(dev(y, z, x, c))

    def pack(p, first, second):
        wsend[p] = jnp.concatenate(
            (first.astype(F32), second.astype(F32)), axis=0
        ).astype(BF16)

    pack(0, wq[:, :HD], wq[:, HD:])
    pack(1, wk[...], wv[...])
    pack(2, wo[:, :HD], wo[:, HD:])
    lane = iota((8, 128), 1)
    spread = jnp.zeros((8, 128), I32)
    for k in range(RESP):
        spread = jnp.where(lane == k, pslot[0:1, k:k + 1], spread)
    slot_out[...] = spread

    xin[...] = jnp.ones((ROWS, WIDE), BF16)
    xin[:, :FEAT] = roll[...]
    slots = NZ * SLOTS
    j = iota((slots, NX * NZ), 0)
    dest = ((j >> 2) & (NX - 1)) * NZ + (j >> 4)
    other = iota((slots, NX * NZ), 1)
    sending = counts[...].astype(F32)
    start = jnp.sum(jnp.where(other < dest, sending, 0.0), axis=1, keepdims=True)
    amount = jnp.sum(jnp.where(other == dest, sending, 0.0), axis=1, keepdims=True)
    k_slot = (iota((slots, 1), 0) & 3).astype(F32)
    wanted = jnp.where((k_slot < amount) & (k_slot < CAP), start + k_slot, -1.0)
    pick = ones_where(wanted == iota((slots, ROWS), 1).astype(F32))
    zsend[...] = dot(pick, xin[...]).astype(BF16).reshape(NZ, SLOTS, WIDE)
    zrecv[z] = zsend[z]

    greeted = NZ - 1 + NX - 1 + NT - 1

    @pl.when(off_diagonal)
    def _():
        pl.semaphore_wait(barrier, greeted + 1)

    @pl.when(jnp.logical_not(off_diagonal))
    def _():
        pl.semaphore_wait(barrier, greeted)

    def z_out(k):
        t = (z + k) % NZ
        return remote(zsend.at[t], zrecv.at[z], za_s.at[k], za_r.at[k], dev(x, t, y, c))

    def z_in(k):
        f = (z + NZ - k) % NZ
        return remote(zsend.at[f], zrecv.at[f], za_s.at[k], za_r.at[k], dev(x, f, y, c))

    def turned(first):
        if first:
            return remote(wsend, wbuf.at[z], tr_s.at[0], tr_r.at[0], dev(y, z, x, c))
        return remote(slot_out, slot_in, tr_s.at[1], tr_r.at[1], dev(y, z, x, c))

    @pl.when(off_diagonal)
    def _():
        turned(True).start()
        turned(False).start()

    @pl.loop(1, NZ)
    def _(k):
        z_out(k).start()

    @pl.when(jnp.logical_not(off_diagonal))
    def _():
        wbuf[z] = wsend[...]
        slot_in[...] = slot_out[...]

    up, down = (z + 1) % NZ, (z + NZ - 1) % NZ

    def ring_block(d, s):
        return (z + NZ - s) % NZ if d == 0 else (z + s) % NZ

    def ring(p, d, s, distance):
        block = wbuf.at[ring_block(d, distance), p]
        return remote(
            block, block, ring_s.at[p, d, s], ring_r.at[p, d, s],
            dev(x, up if d == 0 else down, y, c),
        )

    def unpack(p, block):
        v = wbuf[block, p].astype(F32)
        at = pl.ds(pl.multiple_of(block * WROWS, 8), WROWS)
        w32[p, at, 0:HD] = v[:WROWS]
        w32[p, at, HD:2 * HD] = v[WROWS:]

    def ring_open(p):
        ring(p, 0, 0, 0).start()
        ring(p, 1, 0, 0).start()
        unpack(p, z)

    def ring_steps(pieces, low, high):
        @pl.loop(low, high)
        def _(s):
            for p in pieces:
                for d in (0, 1):
                    ring(p, d, s - 1, s).wait_recv()
                    ring(p, d, s, s).start()
            for p in pieces:
                for d in (0, 1):
                    unpack(p, ring_block(d, s))

    def ring_close(pieces):
        last = NZ // 2
        for p in pieces:
            for d in (0, 1):
                ring(p, d, last - 2, last - 1).wait_recv()
            ring(p, 0, last - 1, last - 1).start()
        for p in pieces:
            for d in (0, 1):
                unpack(p, ring_block(d, last - 1))
        for p in pieces:
            ring(p, 0, last - 1, last).wait_recv()
            unpack(p, ring_block(0, last))

    @pl.when(off_diagonal)
    def _():
        turned(True).wait_recv()
        turned(False).wait_recv()

    ring_open(0)
    ring_open(1)
    ring_steps((0, 1), 1, 3)

    @pl.loop(1, NZ)
    def _(k):
        z_in(k).wait_recv()

    i = iota((ALL_SLOTS, slots), 0)
    q = (i * 171) >> 9
    held_at = (q & (NZ - 1)) * SLOTS + (q >> 4) * 4 + (i - 3 * q)
    squeeze = ones_where(held_at == iota((ALL_SLOTS, slots), 1))
    xg[x] = dot(squeeze, zrecv[...].reshape(slots, WIDE)).astype(BF16)

    right, left = (x + 1) % NX, (x + NX - 1) % NX
    parts = (pl.ds(0, HALF), pl.ds(HALF, HALF))
    plan = (
        (0, 0, 1), (0, 1, 1), (1, 1, 1), (1, 0, 1), (0, 0, 2), (1, 1, 2),
    )

    def x_block(d, distance):
        return (x + NX - distance) % NX if d == 0 else (x + distance) % NX

    def x_out(n):
        d, half, distance = plan[n]
        block = xg.at[x_block(d, distance - 1), parts[half]]
        return remote(
            block, block, xg_s.at[n], xg_r.at[n],
            dev(right if d == 0 else left, z, y, c),
        )

    def x_in(n):
        d, half, distance = plan[n]
        block = xg.at[x_block(d, distance), parts[half]]
        return remote(
            block, block, xg_s.at[n], xg_r.at[n],
            dev(right if d == 0 else left, z, y, c),
        )

    for n in (0, 2, 1, 3):
        x_out(n).start()
    x_in(0).wait_recv()
    x_out(4).start()
    x_in(2).wait_recv()
    x_out(5).start()
    ring_steps((0, 1), 3, 5)
    for n in (1, 3, 4, 5):
        x_in(n).wait_recv()

    before = ones_where(iota((ALL_SLOTS, ALL_SLOTS), 0) < iota((ALL_SLOTS, ALL_SLOTS), 1))
    flag_lane = ones_where(iota((16, 128), 1) == FEAT - 512)
    my_gain = gain[pl.ds(ten, 1), :]
    table = jnp.zeros((8, 128), F32)
    sub = iota((8, 128), 0)

    def share(dx):
        return remote(
            xs.at[c, dx], xs.at[c, dx], cs_s.at[dx], cs_r.at[dx], dev(x, z, y, 1 - c)
        )

    def share_in(dx):
        return remote(
            xs.at[1 - c, dx], xs.at[1 - c, dx], cs_s.at[dx], cs_r.at[dx], dev(x, z, y, 1 - c)
        )

    for dx in range(NX):
        s = xg[:, dx * KEPT:(dx + 1) * KEPT, :].reshape(ALL_SLOTS, WIDE)
        filled = dot(flag_lane, s[:, 512:WIDE], NTR)
        rank = dot(filled.astype(BF16), before)
        key = jnp.where(filled > 0.5, rank, -1.0)[0:1]
        place = ones_where(iota((ROWS, ALL_SLOTS), 0).astype(F32) == key)
        rows = dot(place, s)[:, :FEAT]
        judged[dx] = rows.astype(BF16)
        xs[c, dx] = (rows * my_gain).astype(BF16)
        share(dx).start()
        squares = column_to_row(jnp.sum(rows * rows, axis=1, keepdims=True))
        table = jnp.where(sub == dx, squares, table)

    sq_in[0] = table

    def squares_out(k):
        return remote(
            sq_in.at[0], sq_in.at[k], sq_s.at[k], sq_r.at[k],
            {"pair": pair, "tensor": (ten + k) % NT},
        )

    @pl.loop(1, NT)
    def _(k):
        squares_out(k).start()

    ring_steps((0, 1), 5, NZ // 2 - 1)
    ring_close((0, 1))
    ring_open(2)
    for dx in range(NX):
        share_in(dx).wait_recv()

    first = xs[0].reshape(NX * ROWS, FEAT)
    second = xs[1].reshape(NX * ROWS, FEAT)
    for p in (0, 1):
        w = w32[p].astype(BF16)
        t = dot(first, w[:FEAT]) + dot(second, w[FEAT:])
        part[:, :, p * 256:(p + 1) * 256] = t.astype(BF16).reshape(NX, ROWS, 256)

    def sum_out(k):
        t = (y + k) % NY
        return remote(part.at[t], part_in.at[k], rs_s.at[k], rs_r.at[k], dev(x, z, t, c))

    def far_out(k):
        t = (y + k) % NY
        return remote(
            part.at[(t + NY // 2) % NY, :, pl.ds(256, 256)], far_in.at[k],
            far_s.at[k], far_r.at[k], dev(x, z, t, c),
        )

    for k in (2, 1, 3):
        sum_out(k).start()
        far_out(k).start()

    ring_steps((2,), 1, 4)

    @pl.loop(1, NT)
    def _(k):
        squares_out(k).wait_recv()

    total = sq_in[0]
    for k in range(1, NT):
        total = total + sq_in[k]
    far_y = (y + NY // 2) % NY
    width = float(NT * FEAT)

    def row_scale(which):
        row = jnp.sum(jnp.where(sub == which, total, 0.0), axis=0, keepdims=True)
        return lax.rsqrt(row_to_column(row, ROWS) / width + epsilon)

    scale_own, scale_far = row_scale(y), row_scale(far_y)
    for k in range(1, NY):
        sum_out(k).wait_recv()
        far_out(k).wait_recv()
    own = part[y].astype(F32)
    far = part[far_y, :, 256:512].astype(F32)
    for k in range(1, NY):
        own = own + part_in[k].astype(F32)
        far = far + far_in[k].astype(F32)
    own = (own * scale_own).astype(BF16)
    far = (far * scale_far).astype(BF16)

    queries = jnp.concatenate((own[:, 0:HD], own[:, HD:2 * HD]), axis=0)
    col = iota((2 * ROWS, ROWS), 1)
    row = iota((2 * ROWS, ROWS), 0)
    row = jnp.where(row >= ROWS, row - ROWS, row)
    resp_q, resp_k = row >> 5, col >> 5
    spot_q, spot_k = row & (LEN - 1), col & (LEN - 1)

    def by_response(resp, values):
        return jnp.where(resp == 0, values[0], jnp.where(resp == 1, values[1], values[2]))

    own_lens = [lens[(y * NZ + z) * RESP + k] for k in range(RESP)]
    far_lens = [lens[(far_y * NZ + z) * RESP + k] for k in range(RESP)]
    partner = by_response(resp_q, [slot_in[0:1, k:k + 1] for k in range(RESP)])
    own_ok = (resp_q == resp_k) & (spot_k <= spot_q) & (spot_k < by_response(resp_k, own_lens))
    far_ok = (partner == resp_k) & (spot_k < by_response(resp_k, far_lens))

    def powers(keys, ok):
        scores = dot(queries, keys, NTR) * score_scale
        scores = soft_cap * jnp.tanh(scores / soft_cap)
        return jnp.exp(jnp.where(ok, scores, negative))

    p_own = powers(own[:, 256:384], own_ok)
    p_far = powers(far[:, 0:HD], far_ok)
    whole = jnp.sum(p_own, axis=1, keepdims=True) + jnp.sum(p_far, axis=1, keepdims=True)
    mixed = dot((p_own / whole).astype(BF16), own[:, 384:512])
    mixed = mixed + dot((p_far / whole).astype(BF16), far[:, HD:2 * HD])
    row = iota((2 * ROWS, HD), 0)
    row = jnp.where(row >= ROWS, row - ROWS, row)
    present = (row & (LEN - 1)) < by_response(row >> 5, own_lens)
    mixed = jnp.where(present, mixed, 0.0).astype(BF16)
    ctx[y] = jnp.concatenate((mixed[:ROWS], mixed[ROWS:]), axis=1)

    def ctx_out(k):
        return remote(ctx.at[y], ctx.at[y], cx_s.at[k], cx_r.at[k], dev(x, z, (y + k) % NY, c))

    def ctx_in(k):
        f = (y + NY - k) % NY
        return remote(ctx.at[f], ctx.at[f], cx_s.at[k], cx_r.at[k], dev(x, z, f, c))

    for k in (2, 1, 3):
        ctx_out(k).start()
    ring_steps((2,), 4, NZ // 2 - 1)
    ring_close((2,))
    for k in range(1, NY):
        ctx_in(k).wait_recv()

    context = ctx[...].reshape(NX * ROWS, 2 * HD)

    def project(half):
        w = w32[2, pl.ds(pl.multiple_of(half * FEAT, 8), FEAT), :].astype(BF16)
        return dot(context, w, NTR).astype(BF16).reshape(NX, ROWS, FEAT)

    co_out[...] = project(1 - c)
    swap = remote(co_out, co_in, co_s.at[0], co_r.at[0], dev(x, z, y, 1 - c))
    swap.start()
    mine = project(c).astype(F32)
    swap.wait_recv()
    xo_out[...] = (mine + co_in[...].astype(F32)).astype(BF16)

    def xsum_out(k):
        t = (x + k) % NX
        return remote(xo_out.at[t], xo_in.at[k], xo_s.at[k], xo_r.at[k], dev(t, z, y, c))

    for k in (2, 1, 3):
        xsum_out(k).start()
    attended = xo_out[x].astype(F32)
    for k in (1, 3, 2):
        xsum_out(k).wait_recv()
        attended = attended + xo_in[k].astype(F32)

    squares = column_to_row(jnp.sum(attended * attended, axis=1, keepdims=True))
    fin_in[0] = jnp.where(sub == 0, squares, 0.0)

    def fin_out(k):
        return remote(
            fin_in.at[0], fin_in.at[k], fn_s.at[k], fn_r.at[k],
            {"pair": pair, "tensor": (ten + k) % NT},
        )

    @pl.loop(1, NT)
    def _(k):
        fin_out(k).start()

    @pl.when(off_diagonal)
    def _():
        turned(True).wait_send()
        turned(False).wait_send()

    @pl.loop(1, NZ)
    def _(k):
        z_out(k).wait_send()

    for p in range(3):
        @pl.loop(0, NZ // 2 - 1)
        def _(s):
            ring(p, 0, s, s).wait_send()
            ring(p, 1, s, s).wait_send()

        ring(p, 0, NZ // 2 - 1, NZ // 2 - 1).wait_send()
    for n in range(6):
        x_out(n).wait_send()
    for dx in range(NX):
        share(dx).wait_send()

    @pl.loop(1, NT)
    def _(k):
        squares_out(k).wait_send()

    for k in range(1, NY):
        sum_out(k).wait_send()
        far_out(k).wait_send()
        ctx_out(k).wait_send()
        xsum_out(k).wait_send()
    swap.wait_send()

    residual = judged[x].astype(F32)
    gained = attended * post[...]

    @pl.loop(1, NT)
    def _(k):
        fin_out(k).wait_recv()

    total = fin_in[0]
    for k in range(1, NT):
        total = total + fin_in[k]
    scale = lax.rsqrt(row_to_column(total[0:1], ROWS) / width + epsilon)
    out[...] = (residual + gained * scale).astype(BF16)

    @pl.loop(1, NT)
    def _(k):
        fin_out(k).wait_send()


def shards(
    rollout, counts, lengths, partner_slot, pre_gain, post_gain,
    query_weight, key_weight, value_weight, out_weight,
):
    vmem = pl.BlockSpec(memory_space=pltpu.VMEM)
    smem = pl.BlockSpec(memory_space=pltpu.SMEM)
    dma = pltpu.SemaphoreType.DMA
    scratch = [
        pltpu.VMEM((ROWS, WIDE), BF16),
        pltpu.VMEM((NZ, SLOTS, WIDE), BF16),
        pltpu.VMEM((NZ, SLOTS, WIDE), BF16),
        pltpu.VMEM((3, 2 * WROWS, HD), BF16),
        pltpu.VMEM((NZ, 3, 2 * WROWS, HD), BF16),
        pltpu.VMEM((3, BLOCK, 2 * HD), F32),
        pltpu.VMEM((8, 128), I32),
        pltpu.VMEM((8, 128), I32),
        pltpu.VMEM((NX, ALL_SLOTS, WIDE), BF16),
        pltpu.VMEM((NC, NX, ROWS, FEAT), BF16),
        pltpu.VMEM((NX, ROWS, FEAT), BF16),
        pltpu.VMEM((NT, 8, 128), F32),
        pltpu.VMEM((NT, 8, 128), F32),
        pltpu.VMEM((NX, ROWS, 512), BF16),
        pltpu.VMEM((NY, ROWS, 512), BF16),
        pltpu.VMEM((NY, ROWS, 256), BF16),
        pltpu.VMEM((NY, ROWS, 256), BF16),
        pltpu.VMEM((NX, ROWS, FEAT), BF16),
        pltpu.VMEM((NX, ROWS, FEAT), BF16),
        pltpu.VMEM((NX, ROWS, FEAT), BF16),
        pltpu.VMEM((NX, ROWS, FEAT), BF16),
        dma((2,)), dma((2,)),
        dma((NZ,)), dma((NZ,)),
        dma((3, 2, NZ // 2)), dma((3, 2, NZ // 2)),
        dma((6,)), dma((6,)),
        dma((NX,)), dma((NX,)),
        dma((NT,)), dma((NT,)),
        dma((NY,)), dma((NY,)),
        dma((NY,)), dma((NY,)),
        dma((NY,)), dma((NY,)),
        dma((1,)), dma((1,)),
        dma((NX,)), dma((NX,)),
        dma((NT,)), dma((NT,)),
    ]
    return pl.pallas_call(
        kernel,
        out_shape=jax.ShapeDtypeStruct((ROWS, FEAT), BF16),
        in_specs=[vmem, vmem, smem] + [vmem] * 7,
        out_specs=vmem,
        scratch_shapes=scratch,
        compiler_params=pltpu.CompilerParams(
            collective_id=0, has_side_effects=True, vmem_limit_bytes=40 * 1024 * 1024
        ),
    )(
        rollout, counts, lengths, partner_slot, pre_gain.reshape(NT, FEAT),
        post_gain.reshape(1, FEAT), query_weight, key_weight, value_weight, out_weight,
    )


def solution(mesh):
    placed = (
        P("pair", "tensor"),
        P("pair", None),
        P(),
        P("pair", None),
        P(),
        P("tensor"),
        P("pair", "tensor"),
        P("pair", "tensor"),
        P("pair", "tensor"),
        P("pair", "tensor"),
    )
    return jax.shard_map(
        shards, mesh=mesh, in_specs=placed, out_specs=P("pair", "tensor"), check_vma=False
    )
```

time: 662 us -> 110 us (0.17)
  waiting for transfers between devices: 568 us -> 0 us
  Pallas kernels: 0 us -> 104 us
  starting transfers between devices: 32.4 us -> 0 us
  blocking collectives: 17.5 us -> 0 us
  between operations: 13.4 us -> 0.04 us
  other arithmetic: 9.44 us -> 0 us
  matrix products: 9.41 us -> 0 us
    all_gather x4 -> x0, waiting for transfers between devices: 457 us -> none  [the longest x1 137 us: shards(): lax.all_gather(out_weight, 'pair', axis=0, tiled=True)]
    pallas_call x0 -> x1, Pallas kernels: none -> 104 us  [shards(): pl.pallas_call(kernel, out_shape=jax.ShapeDtypeStruct((ROWS, FEAT), BF16)...]
    psum x1 -> x0, waiting for transfers between devices: 80.3 us -> none  [shards(): lax.psum(partial_sum.astype(jnp.bfloat16), 'tensor').astype(jnp.float32)]
    all_to_all x2 -> x0, starting transfers between devices: 28.4 us -> none  [the longest x1 19.1 us: shards(): lax.all_to_all(sending.reshape(pair_count, 1), 'pair', split_axis=0, conc...]
    all_to_all x2 -> x0, waiting for transfers between devices: 25.1 us -> none  [the longest x1 19.8 us: shards(): lax.all_to_all(bucket, 'pair', split_axis=0, concat_axis=0, tiled=True)]
    all_gather x1 -> x0, blocking collectives: 17.5 us -> none  [shards(): wide_rows = lax.all_gather(relaid, 'tensor', axis=1, tiled=True)]
    dot_general x6 -> x0, matrix products: 9.41 us -> none  [the longest x1 3.42 us: shards(): lax.dot_general(context, full_out, (((1,), (1,)), ((), ())), preferred_el...]
  transfers between devices with their start and end apart: 8 -> 0, of which waited for: 8 -> 0; matrix products, arithmetic and copies ran while one was open for 3% -> 0% of each run, Pallas kernels for 0% -> 0%
where the time goes in v1:
time: 110 us; the launch traced here: 109 us
  Pallas kernels  104 us (95%)
  local copies, waits for them, and re-layouts  5.31 us (5%)
    pallas_call x1, Pallas kernels, shards(): pl.pallas_call(kernel, out_shape=jax.ShapeDtypeStruct((ROWS, FEAT), BF16)...  104 us
    unnamed x17, local copies, waits for them, and re-layouts  3.77 us

profile of v1, /device:TPU:1, one launch (start us, length us, event | category | flops | bytes accessed | tf_op | source)
XLA Modules:
  0.0 109.4 jit_solution(490677235954629772)
XLA Ops:
  0.0 0.0 copy-start.1
  0.0 0.7 reshape.7.post
  0.7 0.0 copy-start.5
  0.7 0.0 copy-start.6
  0.7 0.0 copy-start.7
  0.7 0.8 reshape.6.gain
  1.5 0.0 copy-done.1
  1.5 0.0 copy-done.5
  1.6 0.0 copy-done.6
  1.6 0.0 copy-done.7
  1.6 0.0 copy-start
  1.6 0.9 copy-done
  2.5 0.0 copy-start.2
  2.5 0.8 copy-done.2
  3.2 0.0 copy-start.3
  3.2 0.7 copy-done.3
  4.0 0.0 copy-start.4
  4.0 0.7 copy-done.4
  4.7 104.0 %shard_map.100 = bf16[96,576]{1,0:T(8,128)(2,1)S(1)} custom-call(bf16[96,576]{1,0:T(8,128)(2,1)S(1)} %copy-done, s32[1,64]{1,0:T(1,128)S(1)} %copy-done.6, s32[192]{0:T(256)S(1)} %copy-done.5, s32[1,3]{1,0:T(1,128)S(1)} %copy-done.7, f32[8,576]{1,0:T(8,128)S(1)} %reshape.6.gain, f32[1,576]{1,0:T(1,128)S(1)} %reshape.7.post, bf16[72,256]{1,0:T(8,128)(2,1)S(1)} %copy-done.1, ...), custom_call_target="tpu_custom_call" | custom-call | tf_op jit(solution)/shard_map/pallas_call | solution.py:543
  108.7 0.7 copy.12
Async XLA Ops:
  0.0 1.5 %copy-start.1 = (bf16[72,256]{1,0:T(8,128)(2,1)S(1)}, bf16[72,256]{1,0:T(8,128)(2,1)}, u32[]{:S(2)}) copy-start(bf16[72,256]{1,0:T(8,128)(2,1)} %wq.1) | copy-start | bytes 110596
  0.7 0.9 copy-start.5
  0.7 0.9 copy-start.6
  0.7 0.9 copy-start.7
  1.6 0.9 copy-start
  2.5 0.8 copy-start.2
  3.2 0.7 copy-start.3
  4.0 0.7 copy-start.4

commit v2 on v1

--- a/solution.py
+++ b/solution.py
@@ -58,8 +58,8 @@
 
 
 def kernel(
-    roll, counts, lens, pslot, gain, post, wq, wk, wv, wo, out,
-    xin, zsend, zrecv, wsend, wbuf, w32, slot_out, slot_in, xg, xs, judged, sq_in, fin_in,
+    roll_h, counts, lens, pslot, gain, post, wq_h, wk_h, wv_h, wo_h, out,
+    roll, wq, wk, wv, wo, in_s, xin, zsend, zrecv, wsend, wbuf, w32, slot_out, slot_in, xg, xs, judged, sq_in, fin_in,
     part, part_in, far_in, ctx, co_out, co_in, xo_out, xo_in,
     tr_s, tr_r, za_s, za_r, ring_s, ring_r, xg_s, xg_r, cs_s, cs_r, sq_s, sq_r,
     rs_s, rs_r, far_s, far_r, cx_s, cx_r, co_s, co_r, xo_s, xo_r, fn_s, fn_r,
@@ -80,6 +80,15 @@
 
     off_diagonal = x != y
 
+    loads = [
+        pltpu.make_async_copy(a, b, in_s.at[n])
+        for n, (a, b) in enumerate(
+            ((roll_h, roll), (wq_h, wq), (wk_h, wk), (wv_h, wv), (wo_h, wo))
+        )
+    ]
+    for load in loads:
+        load.start()
+
     barrier = pltpu.get_barrier_semaphore()
 
     def greet(where):
@@ -100,6 +109,9 @@
     @pl.when(off_diagonal)
     def _():
         greet(dev(y, z, x, c))
+
+    for load in loads:
+        load.wait()
 
     def pack(p, first, second):
         wsend[p] = jnp.concatenate(
@@ -158,9 +170,12 @@
         turned(True).start()
         turned(False).start()
 
-    @pl.loop(1, NZ)
-    def _(k):
-        z_out(k).start()
+    z_out(NZ // 2).start()
+
+    @pl.loop(1, NZ // 2)
+    def _(k):
+        z_out(NZ // 2 - k).start()
+        z_out(NZ // 2 + k).start()
 
     @pl.when(jnp.logical_not(off_diagonal))
     def _():
@@ -201,8 +216,9 @@
                 for d in (0, 1):
                     unpack(p, ring_block(d, s))
 
-    def ring_close(pieces):
-        last = NZ // 2
+    last = NZ // 2
+
+    def ring_last_sends(pieces):
         for p in pieces:
             for d in (0, 1):
                 ring(p, d, last - 2, last - 1).wait_recv()
@@ -210,6 +226,8 @@
         for p in pieces:
             for d in (0, 1):
                 unpack(p, ring_block(d, last - 1))
+
+    def ring_close(pieces):
         for p in pieces:
             ring(p, 0, last - 1, last).wait_recv()
             unpack(p, ring_block(0, last))
@@ -219,9 +237,10 @@
         turned(True).wait_recv()
         turned(False).wait_recv()
 
-    ring_open(0)
-    ring_open(1)
-    ring_steps((0, 1), 1, 3)
+    early, late = (0, 1), (2,)
+    for p in early:
+        ring_open(p)
+    ring_steps(early, 1, 3)
 
     @pl.loop(1, NZ)
     def _(k):
@@ -260,17 +279,20 @@
 
     for n in (0, 2, 1, 3):
         x_out(n).start()
+    ring_steps(early, 3, 4)
     x_in(0).wait_recv()
     x_out(4).start()
     x_in(2).wait_recv()
     x_out(5).start()
-    ring_steps((0, 1), 3, 5)
+    ring_steps(early, 4, 6)
+    ring_open(2)
     for n in (1, 3, 4, 5):
         x_in(n).wait_recv()
 
     before = ones_where(iota((ALL_SLOTS, ALL_SLOTS), 0) < iota((ALL_SLOTS, ALL_SLOTS), 1))
     flag_lane = ones_where(iota((16, 128), 1) == FEAT - 512)
-    my_gain = gain[pl.ds(ten, 1), :]
+    my_gain = gain[pl.ds(pl.multiple_of(y * NC * FEAT, 128), NC * FEAT)].reshape(1, NC * FEAT)
+    my_gain = jnp.where(c == 0, my_gain[:, :FEAT], my_gain[:, FEAT:])
     table = jnp.zeros((8, 128), F32)
     sub = iota((8, 128), 0)
 
@@ -309,9 +331,11 @@
     def _(k):
         squares_out(k).start()
 
-    ring_steps((0, 1), 5, NZ // 2 - 1)
-    ring_close((0, 1))
-    ring_open(2)
+    ring_steps(early, 6, last - 1)
+    ring_steps(late, 1, 2)
+    ring_last_sends(early)
+    ring_steps(late, 2, 3)
+    ring_close(early)
     for dx in range(NX):
         share_in(dx).wait_recv()
 
@@ -337,7 +361,7 @@
         sum_out(k).start()
         far_out(k).start()
 
-    ring_steps((2,), 1, 4)
+    ring_steps(late, 3, 6)
 
     @pl.loop(1, NT)
     def _(k):
@@ -406,33 +430,45 @@
 
     for k in (2, 1, 3):
         ctx_out(k).start()
-    ring_steps((2,), 4, NZ // 2 - 1)
-    ring_close((2,))
-    for k in range(1, NY):
-        ctx_in(k).wait_recv()
-
-    context = ctx[...].reshape(NX * ROWS, 2 * HD)
-
-    def project(half):
-        w = w32[2, pl.ds(pl.multiple_of(half * FEAT, 8), FEAT), :].astype(BF16)
-        return dot(context, w, NTR).astype(BF16).reshape(NX, ROWS, FEAT)
-
-    co_out[...] = project(1 - c)
-    swap = remote(co_out, co_in, co_s.at[0], co_r.at[0], dev(x, z, y, 1 - c))
-    swap.start()
-    mine = project(c).astype(F32)
-    swap.wait_recv()
-    xo_out[...] = (mine + co_in[...].astype(F32)).astype(BF16)
-
-    def xsum_out(k):
+    ring_steps(late, 6, last - 1)
+    ring_last_sends(late)
+    ring_close(late)
+
+    def out_rows(half):
+        return w32[2, pl.ds(pl.multiple_of(half * FEAT, 8), FEAT), :].astype(BF16)
+
+    w_other, w_mine = out_rows(1 - c), out_rows(c)
+
+    def swap(k):
+        t = (y + NY - k) % NY
+        return remote(
+            co_out.at[t], co_in.at[t], co_s.at[k], co_r.at[k], dev(x, z, y, 1 - c)
+        )
+
+    def xsum(k):
         t = (x + k) % NX
         return remote(xo_out.at[t], xo_in.at[k], xo_s.at[k], xo_r.at[k], dev(t, z, y, c))
 
-    for k in (2, 1, 3):
-        xsum_out(k).start()
+    order = (0, 1, 3, 2)
+    for k in order:
+        t = (y + NY - k) % NY
+        if k > 0:
+            ctx_in(k).wait_recv()
+        co_out[t] = dot(ctx[t], w_other, NTR).astype(BF16)
+        swap(k).start()
+        xo_out[t] = dot(ctx[t], w_mine, NTR).astype(BF16)
+    for k in order:
+        t = (y + NY - k) % NY
+        swap(k).wait_recv()
+        xo_out[t] = (xo_out[t].astype(F32) + co_in[t].astype(F32)).astype(BF16)
+
+        @pl.when(t != x)
+        def _():
+            xsum((t + NX - x) % NX).start()
+
     attended = xo_out[x].astype(F32)
     for k in (1, 3, 2):
-        xsum_out(k).wait_recv()
+        xsum(k).wait_recv()
         attended = attended + xo_in[k].astype(F32)
 
     squares = column_to_row(jnp.sum(attended * attended, axis=1, keepdims=True))
@@ -477,11 +513,12 @@
         sum_out(k).wait_send()
         far_out(k).wait_send()
         ctx_out(k).wait_send()
-        xsum_out(k).wait_send()
-    swap.wait_send()
+        xsum(k).wait_send()
+    for k in order:
+        swap(k).wait_send()
 
     residual = judged[x].astype(F32)
-    gained = attended * post[...]
+    gained = attended * post[...].reshape(1, FEAT)
 
     @pl.loop(1, NT)
     def _(k):
@@ -503,9 +540,16 @@
     query_weight, key_weight, value_weight, out_weight,
 ):
     vmem = pl.BlockSpec(memory_space=pltpu.VMEM)
+    hbm = pl.BlockSpec(memory_space=pltpu.HBM)
     smem = pl.BlockSpec(memory_space=pltpu.SMEM)
     dma = pltpu.SemaphoreType.DMA
     scratch = [
+        pltpu.VMEM((ROWS, FEAT), BF16),
+        pltpu.VMEM((WROWS, 256), BF16),
+        pltpu.VMEM((WROWS, HD), BF16),
+        pltpu.VMEM((WROWS, HD), BF16),
+        pltpu.VMEM((WROWS, 256), BF16),
+        dma((5,)),
         pltpu.VMEM((ROWS, WIDE), BF16),
         pltpu.VMEM((NZ, SLOTS, WIDE), BF16),
         pltpu.VMEM((NZ, SLOTS, WIDE), BF16),
@@ -536,22 +580,22 @@
         dma((NY,)), dma((NY,)),
         dma((NY,)), dma((NY,)),
         dma((NY,)), dma((NY,)),
-        dma((1,)), dma((1,)),
+        dma((NX,)), dma((NX,)),
         dma((NX,)), dma((NX,)),
         dma((NT,)), dma((NT,)),
     ]
     return pl.pallas_call(
         kernel,
         out_shape=jax.ShapeDtypeStruct((ROWS, FEAT), BF16),
-        in_specs=[vmem, vmem, smem] + [vmem] * 7,
+        in_specs=[hbm, vmem, smem, vmem, vmem, vmem, hbm, hbm, hbm, hbm],
         out_specs=vmem,
         scratch_shapes=scratch,
         compiler_params=pltpu.CompilerParams(
-            collective_id=0, has_side_effects=True, vmem_limit_bytes=40 * 1024 * 1024
+            collective_id=0, has_side_effects=True, vmem_limit_bytes=62 * 1024 * 1024
         ),
     )(
-        rollout, counts, lengths, partner_slot, pre_gain.reshape(NT, FEAT),
-        post_gain.reshape(1, FEAT), query_weight, key_weight, value_weight, out_weight,
+        rollout, counts, lengths, partner_slot, pre_gain,
+        post_gain, query_weight, key_weight, value_weight, out_weight,
     )
 
 

time: 110 us -> 96.2 us (0.87)
  Pallas kernels: 104 us -> 94.4 us
  local copies, waits for them, and re-layouts: 5.31 us -> 1.56 us
    pallas_call x1, Pallas kernels: 104 us -> 94.4 us  [shards(): pl.pallas_call(kernel, out_shape=jax.ShapeDtypeStruct((ROWS, FEAT), BF16)...]
    unnamed x17 -> x1, local copies, waits for them, and re-layouts: 3.77 us -> 1.56 us
    reshape x2 -> x0, local copies, waits for them, and re-layouts: 1.53 us -> none  [the longest x1 0.84 us: shards(): pre_gain.reshape(NT, FEAT)]
where the time goes in v2:
time: 96.2 us; the launch traced here: 96 us
  Pallas kernels  94.4 us (98%)
  local copies, waits for them, and re-layouts  1.56 us (2%)
    pallas_call x1, Pallas kernels, shards(): pl.pallas_call(kernel, out_shape=jax.ShapeDtypeStruct((ROWS, FEAT), BF16)...  94.4 us

profile of v2, /device:TPU:1, one launch (start us, length us, event | category | flops | bytes accessed | tf_op | source)
XLA Modules:
  0.0 96.0 jit_solution(10536297674270947669)
XLA Ops:
  0.0 94.4 %shard_map.100 = bf16[96,576]{1,0:T(8,128)(2,1)} custom-call(bf16[96,576]{1,0:T(8,128)(2,1)} %roll_h.1, s32[1,64]{1,0:T(1,128)} %counts.1, s32[192]{0:T(256)} %lens.1, s32[1,3]{1,0:T(1,128)} %pslot.1, f32[4608]{0:T(1024)} %gain.1, f32[576]{0:T(1024)} %post.1, bf16[72,256]{1,0:T(8,128)(2,1)} %wq_h.1, bf16[72,128]{1,0:T(8,128)(2,1)} %wk_h.1, ...), custom_call_target="tpu_custom_call" | custom-call | tf_op jit(solution)/shard_map/pallas_call | solution.py:587
  94.4 1.6 %copy.12 = bf16[96,576]{1,0:T(8,128)(2,1)} copy(bf16[96,576]{1,0:T(8,128)(2,1)} %shard_map.100) | data formatting | bytes 221184

commit v3 on v2

--- a/solution.py
+++ b/solution.py
@@ -110,25 +110,7 @@
     def _():
         greet(dev(y, z, x, c))
 
-    for load in loads:
-        load.wait()
-
-    def pack(p, first, second):
-        wsend[p] = jnp.concatenate(
-            (first.astype(F32), second.astype(F32)), axis=0
-        ).astype(BF16)
-
-    pack(0, wq[:, :HD], wq[:, HD:])
-    pack(1, wk[...], wv[...])
-    pack(2, wo[:, :HD], wo[:, HD:])
-    lane = iota((8, 128), 1)
-    spread = jnp.zeros((8, 128), I32)
-    for k in range(RESP):
-        spread = jnp.where(lane == k, pslot[0:1, k:k + 1], spread)
-    slot_out[...] = spread
-
     xin[...] = jnp.ones((ROWS, WIDE), BF16)
-    xin[:, :FEAT] = roll[...]
     slots = NZ * SLOTS
     j = iota((slots, NX * NZ), 0)
     dest = ((j >> 2) & (NX - 1)) * NZ + (j >> 4)
@@ -139,8 +121,27 @@
     k_slot = (iota((slots, 1), 0) & 3).astype(F32)
     wanted = jnp.where((k_slot < amount) & (k_slot < CAP), start + k_slot, -1.0)
     pick = ones_where(wanted == iota((slots, ROWS), 1).astype(F32))
+    loads[0].wait()
+    xin[:, :FEAT] = roll[...]
     zsend[...] = dot(pick, xin[...]).astype(BF16).reshape(NZ, SLOTS, WIDE)
     zrecv[z] = zsend[z]
+
+    for load in loads[1:]:
+        load.wait()
+
+    def pack(p, first, second):
+        wsend[p] = jnp.concatenate(
+            (first.astype(F32), second.astype(F32)), axis=0
+        ).astype(BF16)
+
+    pack(0, wq[:, :HD], wq[:, HD:])
+    pack(1, wk[...], wv[...])
+    pack(2, wo[:, :HD], wo[:, HD:])
+    lane = iota((8, 128), 1)
+    spread = jnp.zeros((8, 128), I32)
+    for k in range(RESP):
+        spread = jnp.where(lane == k, pslot[0:1, k:k + 1], spread)
+    slot_out[...] = spread
 
     greeted = NZ - 1 + NX - 1 + NT - 1
 
@@ -237,10 +238,10 @@
         turned(True).wait_recv()
         turned(False).wait_recv()
 
-    early, late = (0, 1), (2,)
-    for p in early:
+    pieces = (0, 1, 2)
+    for p in pieces:
         ring_open(p)
-    ring_steps(early, 1, 3)
+    ring_steps(pieces, 1, 3)
 
     @pl.loop(1, NZ)
     def _(k):
@@ -279,13 +280,12 @@
 
     for n in (0, 2, 1, 3):
         x_out(n).start()
-    ring_steps(early, 3, 4)
+    ring_steps(pieces, 3, 4)
     x_in(0).wait_recv()
     x_out(4).start()
     x_in(2).wait_recv()
     x_out(5).start()
-    ring_steps(early, 4, 6)
-    ring_open(2)
+    ring_steps(pieces, 4, 6)
     for n in (1, 3, 4, 5):
         x_in(n).wait_recv()
 
@@ -331,11 +331,9 @@
     def _(k):
         squares_out(k).start()
 
-    ring_steps(early, 6, last - 1)
-    ring_steps(late, 1, 2)
-    ring_last_sends(early)
-    ring_steps(late, 2, 3)
-    ring_close(early)
+    ring_steps(pieces, 6, last - 1)
+    ring_last_sends(pieces)
+    ring_close((0, 1))
     for dx in range(NX):
         share_in(dx).wait_recv()
 
@@ -361,7 +359,7 @@
         sum_out(k).start()
         far_out(k).start()
 
-    ring_steps(late, 3, 6)
+    ring_close((2,))
 
     @pl.loop(1, NT)
     def _(k):
@@ -430,9 +428,6 @@
 
     for k in (2, 1, 3):
         ctx_out(k).start()
-    ring_steps(late, 6, last - 1)
-    ring_last_sends(late)
-    ring_close(late)
 
     def out_rows(half):
         return w32[2, pl.ds(pl.multiple_of(half * FEAT, 8), FEAT), :].astype(BF16)

time: 96.2 us -> 91 us (0.946)
  Pallas kernels: 94.4 us -> 89.2 us
    pallas_call x1, Pallas kernels: 94.4 us -> 89.2 us  [shards(): pl.pallas_call(kernel, out_shape=jax.ShapeDtypeStruct((ROWS, FEAT), BF16)...]
where the time goes in v3:
time: 91 us; the launch traced here: 90.8 us
  Pallas kernels  89.2 us (98%)
  local copies, waits for them, and re-layouts  1.56 us (2%)
    pallas_call x1, Pallas kernels, shards(): pl.pallas_call(kernel, out_shape=jax.ShapeDtypeStruct((ROWS, FEAT), BF16)...  89.2 us

profile of v3, /device:TPU:1, one launch (start us, length us, event | category | flops | bytes accessed | tf_op | source)
XLA Modules:
  0.0 90.8 jit_solution(3587770059081019602)
XLA Ops:
  0.0 89.2 %shard_map.100 = bf16[96,576]{1,0:T(8,128)(2,1)} custom-call(bf16[96,576]{1,0:T(8,128)(2,1)} %roll_h.1, s32[1,64]{1,0:T(1,128)} %counts.1, s32[192]{0:T(256)} %lens.1, s32[1,3]{1,0:T(1,128)} %pslot.1, f32[4608]{0:T(1024)} %gain.1, f32[576]{0:T(1024)} %post.1, bf16[72,256]{1,0:T(8,128)(2,1)} %wq_h.1, bf16[72,128]{1,0:T(8,128)(2,1)} %wk_h.1, ...), custom_call_target="tpu_custom_call" | custom-call | tf_op jit(solution)/shard_map/pallas_call | solution.py:582
  89.2 1.6 %copy.12 = bf16[96,576]{1,0:T(8,128)(2,1)} copy(bf16[96,576]{1,0:T(8,128)(2,1)} %shard_map.100) | data formatting | bytes 221184

commit v4 on v3

--- a/solution.py
+++ b/solution.py
@@ -60,9 +60,9 @@
 def kernel(
     roll_h, counts, lens, pslot, gain, post, wq_h, wk_h, wv_h, wo_h, out,
     roll, wq, wk, wv, wo, in_s, xin, zsend, zrecv, wsend, wbuf, w32, slot_out, slot_in, xg, xs, judged, sq_in, fin_in,
-    part, part_in, far_in, ctx, co_out, co_in, xo_out, xo_in,
+    part, part_in, ycomb, ctx, co_out, co_in, xo_out, xo_in, xcomb,
     tr_s, tr_r, za_s, za_r, ring_s, ring_r, xg_s, xg_r, cs_s, cs_r, sq_s, sq_r,
-    rs_s, rs_r, far_s, far_r, cx_s, cx_r, co_s, co_r, xo_s, xo_r, fn_s, fn_r,
+    rs_s, rs_r, cx_s, cx_r, co_s, co_r, xo_s, xo_r, fn_s, fn_r,
 ):
     pair = lax.axis_index("pair")
     ten = lax.axis_index("tensor")
@@ -339,25 +339,40 @@
 
     first = xs[0].reshape(NX * ROWS, FEAT)
     second = xs[1].reshape(NX * ROWS, FEAT)
-    for p in (0, 1):
+
+    def products(p):
         w = w32[p].astype(BF16)
         t = dot(first, w[:FEAT]) + dot(second, w[FEAT:])
-        part[:, :, p * 256:(p + 1) * 256] = t.astype(BF16).reshape(NX, ROWS, 256)
-
-    def sum_out(k):
-        t = (y + k) % NY
-        return remote(part.at[t], part_in.at[k], rs_s.at[k], rs_r.at[k], dev(x, z, t, c))
-
-    def far_out(k):
-        t = (y + k) % NY
-        return remote(
-            part.at[(t + NY // 2) % NY, :, pl.ds(256, 256)], far_in.at[k],
-            far_s.at[k], far_r.at[k], dev(x, z, t, c),
-        )
-
-    for k in (2, 1, 3):
-        sum_out(k).start()
-        far_out(k).start()
+        return t.astype(BF16).reshape(NX, ROWS, 256)
+
+    key_values = products(1)
+    part[:, :, 256:512] = key_values
+    for dx in range(NX):
+        part[dx, :, 512:768] = key_values[(dx + NX // 2) % NX]
+    part[:, :, 0:256] = products(0)
+
+    halves = (pl.ds(0, ROWS // 2), pl.ds(ROWS // 2, ROWS // 2))
+
+    def y_near(d):
+        return (y + 1) % NY if d == 0 else (y + NY - 1) % NY
+
+    def ysum(stage, d):
+        t = y_near(d)
+        src = (
+            part.at[(y + NY // 2) % NY, halves[d]], part.at[t, halves[1 - d]], ycomb.at[d]
+        )[stage]
+        return remote(
+            src, part_in.at[stage, d], rs_s.at[stage, d], rs_r.at[stage, d], dev(x, z, t, c)
+        )
+
+    for stage in (0, 1):
+        for d in (0, 1):
+            ysum(stage, d).start()
+    for d in (0, 1):
+        ysum(0, d).wait_recv()
+        mine = part[y_near(d), halves[d]].astype(F32)
+        ycomb[d] = (mine + part_in[0, d].astype(F32)).astype(BF16)
+        ysum(2, d).start()
 
     ring_close((2,))
 
@@ -376,14 +391,17 @@
         return lax.rsqrt(row_to_column(row, ROWS) / width + epsilon)
 
     scale_own, scale_far = row_scale(y), row_scale(far_y)
-    for k in range(1, NY):
-        sum_out(k).wait_recv()
-        far_out(k).wait_recv()
-    own = part[y].astype(F32)
-    far = part[far_y, :, 256:512].astype(F32)
-    for k in range(1, NY):
-        own = own + part_in[k].astype(F32)
-        far = far + far_in[k].astype(F32)
+    for stage in (1, 2):
+        for d in (0, 1):
+            ysum(stage, d).wait_recv()
+    both = part[y].astype(F32) + jnp.concatenate(
+        (
+            part_in[2, 0].astype(F32) + part_in[1, 1].astype(F32),
+            part_in[2, 1].astype(F32) + part_in[1, 0].astype(F32),
+        ),
+        axis=0,
+    )
+    own, far = both[:, 0:512], both[:, 512:768]
     own = (own * scale_own).astype(BF16)
     far = (far * scale_far).astype(BF16)
 
@@ -434,37 +452,57 @@
 
     w_other, w_mine = out_rows(1 - c), out_rows(c)
 
-    def swap(k):
-        t = (y + NY - k) % NY
-        return remote(
-            co_out.at[t], co_in.at[t], co_s.at[k], co_r.at[k], dev(x, z, y, 1 - c)
-        )
-
-    def xsum(k):
-        t = (x + k) % NX
-        return remote(xo_out.at[t], xo_in.at[k], xo_s.at[k], xo_r.at[k], dev(t, z, y, c))
-
-    order = (0, 1, 3, 2)
-    for k in order:
+    def swap(t):
+        return remote(
+            co_out.at[t], co_in.at[t], co_s.at[t], co_r.at[t], dev(x, z, y, 1 - c)
+        )
+
+    for k in (0, 1, 3, 2):
         t = (y + NY - k) % NY
         if k > 0:
             ctx_in(k).wait_recv()
         co_out[t] = dot(ctx[t], w_other, NTR).astype(BF16)
-        swap(k).start()
+        swap(t).start()
         xo_out[t] = dot(ctx[t], w_mine, NTR).astype(BF16)
-    for k in order:
-        t = (y + NY - k) % NY
-        swap(k).wait_recv()
+
+    def x_near(d):
+        return right if d == 0 else left
+
+    def xsum(stage, d):
+        t = x_near(d)
+        src = (
+            xo_out.at[(x + NX // 2) % NX, halves[d]], xo_out.at[t, halves[1 - d]], xcomb.at[d]
+        )[stage]
+        return remote(
+            src, xo_in.at[stage, d], xo_s.at[stage, d], xo_r.at[stage, d], dev(t, z, y, c)
+        )
+
+    def swapped(t):
+        swap(t).wait_recv()
         xo_out[t] = (xo_out[t].astype(F32) + co_in[t].astype(F32)).astype(BF16)
 
-        @pl.when(t != x)
-        def _():
-            xsum((t + NX - x) % NX).start()
-
-    attended = xo_out[x].astype(F32)
-    for k in (1, 3, 2):
-        xsum(k).wait_recv()
-        attended = attended + xo_in[k].astype(F32)
+    swapped((x + NX // 2) % NX)
+    for d in (0, 1):
+        xsum(0, d).start()
+    for d in (0, 1):
+        swapped(x_near(d))
+        xsum(1, d).start()
+    swapped(x)
+    for d in (0, 1):
+        xsum(0, d).wait_recv()
+        mine = xo_out[x_near(d), halves[d]].astype(F32)
+        xcomb[d] = (mine + xo_in[0, d].astype(F32)).astype(BF16)
+        xsum(2, d).start()
+    for stage in (1, 2):
+        for d in (0, 1):
+            xsum(stage, d).wait_recv()
+    attended = xo_out[x].astype(F32) + jnp.concatenate(
+        (
+            xo_in[2, 0].astype(F32) + xo_in[1, 1].astype(F32),
+            xo_in[2, 1].astype(F32) + xo_in[1, 0].astype(F32),
+        ),
+        axis=0,
+    )
 
     squares = column_to_row(jnp.sum(attended * attended, axis=1, keepdims=True))
     fin_in[0] = jnp.where(sub == 0, squares, 0.0)
@@ -504,13 +542,14 @@
     def _(k):
         squares_out(k).wait_send()
 
+    for stage in range(3):
+        for d in (0, 1):
+            ysum(stage, d).wait_send()
+            xsum(stage, d).wait_send()
     for k in range(1, NY):
-        sum_out(k).wait_send()
-        far_out(k).wait_send()
         ctx_out(k).wait_send()
-        xsum(k).wait_send()
-    for k in order:
-        swap(k).wait_send()
+    for t in range(NX):
+        swap(t).wait_send()
 
     residual = judged[x].astype(F32)
     gained = attended * post[...].reshape(1, FEAT)
@@ -558,25 +597,25 @@
         pltpu.VMEM((NX, ROWS, FEAT), BF16),
         pltpu.VMEM((NT, 8, 128), F32),
         pltpu.VMEM((NT, 8, 128), F32),
-        pltpu.VMEM((NX, ROWS, 512), BF16),
-        pltpu.VMEM((NY, ROWS, 512), BF16),
-        pltpu.VMEM((NY, ROWS, 256), BF16),
+        pltpu.VMEM((NX, ROWS, 768), BF16),
+        pltpu.VMEM((3, 2, ROWS // 2, 768), BF16),
+        pltpu.VMEM((2, ROWS // 2, 768), BF16),
         pltpu.VMEM((NY, ROWS, 256), BF16),
         pltpu.VMEM((NX, ROWS, FEAT), BF16),
         pltpu.VMEM((NX, ROWS, FEAT), BF16),
         pltpu.VMEM((NX, ROWS, FEAT), BF16),
-        pltpu.VMEM((NX, ROWS, FEAT), BF16),
+        pltpu.VMEM((3, 2, ROWS // 2, FEAT), BF16),
+        pltpu.VMEM((2, ROWS // 2, FEAT), BF16),
         dma((2,)), dma((2,)),
         dma((NZ,)), dma((NZ,)),
         dma((3, 2, NZ // 2)), dma((3, 2, NZ // 2)),
         dma((6,)), dma((6,)),
         dma((NX,)), dma((NX,)),
         dma((NT,)), dma((NT,)),
-        dma((NY,)), dma((NY,)),
-        dma((NY,)), dma((NY,)),
+        dma((3, 2)), dma((3, 2)),
         dma((NY,)), dma((NY,)),
         dma((NX,)), dma((NX,)),
-        dma((NX,)), dma((NX,)),
+        dma((3, 2)), dma((3, 2)),
         dma((NT,)), dma((NT,)),
     ]
     return pl.pallas_call(

time: 91 us -> 92.1 us (1.012)
  Pallas kernels: 89.2 us -> 90.3 us
    pallas_call x1, Pallas kernels: 89.2 us -> 90.3 us  [shards(): pl.pallas_call(kernel, out_shape=jax.ShapeDtypeStruct((ROWS, FEAT), BF16)...]
where the time goes in v4:
time: 92.1 us; the launch traced here: 91.9 us
  Pallas kernels  90.3 us (98%)
  local copies, waits for them, and re-layouts  1.56 us (2%)
    pallas_call x1, Pallas kernels, shards(): pl.pallas_call(kernel, out_shape=jax.ShapeDtypeStruct((ROWS, FEAT), BF16)...  90.3 us

profile of v4, /device:TPU:1, one launch (start us, length us, event | category | flops | bytes accessed | tf_op | source)
XLA Modules:
  0.0 91.9 jit_solution(14584368761729445639)
XLA Ops:
  0.0 90.3 %shard_map.100 = bf16[96,576]{1,0:T(8,128)(2,1)} custom-call(bf16[96,576]{1,0:T(8,128)(2,1)} %roll_h.1, s32[1,64]{1,0:T(1,128)} %counts.1, s32[192]{0:T(256)} %lens.1, s32[1,3]{1,0:T(1,128)} %pslot.1, f32[4608]{0:T(1024)} %gain.1, f32[576]{0:T(1024)} %post.1, bf16[72,256]{1,0:T(8,128)(2,1)} %wq_h.1, bf16[72,128]{1,0:T(8,128)(2,1)} %wk_h.1, ...), custom_call_target="tpu_custom_call" | custom-call | tf_op jit(solution)/shard_map/pallas_call | solution.py:621
  90.3 1.6 %copy.12 = bf16[96,576]{1,0:T(8,128)(2,1)} copy(bf16[96,576]{1,0:T(8,128)(2,1)} %shard_map.100) | data formatting | bytes 221184

commit v5 on v3

--- a/solution.py
+++ b/solution.py
@@ -12,7 +12,9 @@
 RESP = 3
 ROWS = RESP * LEN
 FEAT = 576
-WIDE = 640
+SIDE = 256
+TAIL = FEAT - 2 * SIDE
+WIDE = SIDE + 128
 WROWS = 72
 BLOCK = NZ * WROWS
 CAP = 3
@@ -59,7 +61,7 @@
 
 def kernel(
     roll_h, counts, lens, pslot, gain, post, wq_h, wk_h, wv_h, wo_h, out,
-    roll, wq, wk, wv, wo, in_s, xin, zsend, zrecv, wsend, wbuf, w32, slot_out, slot_in, xg, xs, judged, sq_in, fin_in,
+    roll, wq, wk, wv, wo, in_s, low, zsend, zrecv, wsend, wbuf, w32, slot_out, slot_in, xg0, xg1, xs, judged, sq_in, fin_in,
     part, part_in, far_in, ctx, co_out, co_in, xo_out, xo_in,
     tr_s, tr_r, za_s, za_r, ring_s, ring_r, xg_s, xg_r, cs_s, cs_r, sq_s, sq_r,
     rs_s, rs_r, far_s, far_r, cx_s, cx_r, co_s, co_r, xo_s, xo_r, fn_s, fn_r,
@@ -110,7 +112,6 @@
     def _():
         greet(dev(y, z, x, c))
 
-    xin[...] = jnp.ones((ROWS, WIDE), BF16)
     slots = NZ * SLOTS
     j = iota((slots, NX * NZ), 0)
     dest = ((j >> 2) & (NX - 1)) * NZ + (j >> 4)
@@ -119,12 +120,30 @@
     start = jnp.sum(jnp.where(other < dest, sending, 0.0), axis=1, keepdims=True)
     amount = jnp.sum(jnp.where(other == dest, sending, 0.0), axis=1, keepdims=True)
     k_slot = (iota((slots, 1), 0) & 3).astype(F32)
-    wanted = jnp.where((k_slot < amount) & (k_slot < CAP), start + k_slot, -1.0)
-    pick = ones_where(wanted == iota((slots, ROWS), 1).astype(F32))
+    spare = k_slot == CAP
+    row_of = iota((slots, ROWS), 1).astype(F32)
+
+    def picking(cond, k):
+        return ones_where(jnp.where(cond & (amount > k), start + k, -1.0) == row_of)
+
+    pick = picking(k_slot < CAP, k_slot)
+    pick_tail = [picking(spare, float(k)) for k in range(CAP)]
+    spot = iota((slots, 128), 1) - TAIL
+    flags = jnp.where(
+        spare & (spot >= 0) & (spot < CAP) & (spot.astype(F32) < amount), 1.0, 0.0
+    )
+    low[...] = jnp.zeros((ROWS, 128), BF16)
     loads[0].wait()
-    xin[:, :FEAT] = roll[...]
-    zsend[...] = dot(pick, xin[...]).astype(BF16).reshape(NZ, SLOTS, WIDE)
-    zrecv[z] = zsend[z]
+    low[:, 0:TAIL] = roll[:, 2 * SIDE:FEAT]
+    low_tail = low[...]
+    high_tail = pltpu.roll(low_tail.astype(F32), TAIL, 1).astype(BF16)
+    base = dot(pick, roll[:, 0:2 * SIDE])
+    tile0 = base[:, 0:128] + dot(pick_tail[0], low_tail) + dot(pick_tail[1], high_tail)
+    tile1 = base[:, 128:256] + dot(pick_tail[2], low_tail) + flags
+    zsend[0] = jnp.concatenate((tile0, tile1), axis=1).astype(BF16).reshape(NZ, SLOTS, SIDE)
+    zsend[1] = base[:, SIDE:].astype(BF16).reshape(NZ, SLOTS, SIDE)
+    for h in (0, 1):
+        zrecv[h, z] = zsend[h, z]
 
     for load in loads[1:]:
         load.wait()
@@ -153,13 +172,17 @@
     def _():
         pl.semaphore_wait(barrier, greeted)
 
-    def z_out(k):
+    def z_out(h, k):
         t = (z + k) % NZ
-        return remote(zsend.at[t], zrecv.at[z], za_s.at[k], za_r.at[k], dev(x, t, y, c))
-
-    def z_in(k):
+        return remote(
+            zsend.at[h, t], zrecv.at[h, z], za_s.at[h, k], za_r.at[h, k], dev(x, t, y, c)
+        )
+
+    def z_in(h, k):
         f = (z + NZ - k) % NZ
-        return remote(zsend.at[f], zrecv.at[f], za_s.at[k], za_r.at[k], dev(x, f, y, c))
+        return remote(
+            zsend.at[h, f], zrecv.at[h, f], za_s.at[h, k], za_r.at[h, k], dev(x, f, y, c)
+        )
 
     def turned(first):
         if first:
@@ -171,12 +194,13 @@
         turned(True).start()
         turned(False).start()
 
-    z_out(NZ // 2).start()
-
-    @pl.loop(1, NZ // 2)
-    def _(k):
-        z_out(NZ // 2 - k).start()
-        z_out(NZ // 2 + k).start()
+    for h in (0, 1):
+        z_out(h, NZ // 2).start()
+
+        @pl.loop(1, NZ // 2)
+        def _(k):
+            z_out(h, NZ // 2 - k).start()
+            z_out(h, NZ // 2 + k).start()
 
     @pl.when(jnp.logical_not(off_diagonal))
     def _():
@@ -241,56 +265,83 @@
     pieces = (0, 1, 2)
     for p in pieces:
         ring_open(p)
-    ring_steps(pieces, 1, 3)
-
-    @pl.loop(1, NZ)
-    def _(k):
-        z_in(k).wait_recv()
-
-    i = iota((ALL_SLOTS, slots), 0)
-    q = (i * 171) >> 9
-    held_at = (q & (NZ - 1)) * SLOTS + (q >> 4) * 4 + (i - 3 * q)
-    squeeze = ones_where(held_at == iota((ALL_SLOTS, slots), 1))
-    xg[x] = dot(squeeze, zrecv[...].reshape(slots, WIDE)).astype(BF16)
+    ring_steps(pieces, 1, 2)
+
+    def z_wait(h):
+        @pl.loop(1, NZ)
+        def _(k):
+            z_in(h, k).wait_recv()
 
     right, left = (x + 1) % NX, (x + NX - 1) % NX
     parts = (pl.ds(0, HALF), pl.ds(HALF, HALF))
     plan = (
         (0, 0, 1), (0, 1, 1), (1, 1, 1), (1, 0, 1), (0, 0, 2), (1, 1, 2),
     )
+    held = (xg0, xg1)
 
     def x_block(d, distance):
         return (x + NX - distance) % NX if d == 0 else (x + distance) % NX
 
-    def x_out(n):
-        d, half, distance = plan[n]
-        block = xg.at[x_block(d, distance - 1), parts[half]]
-        return remote(
-            block, block, xg_s.at[n], xg_r.at[n],
+    def x_copy(h, n, distance):
+        d, half, _ = plan[n]
+        block = held[h].at[x_block(d, distance), parts[half]]
+        return remote(
+            block, block, xg_s.at[h, n], xg_r.at[h, n],
             dev(right if d == 0 else left, z, y, c),
         )
 
-    def x_in(n):
-        d, half, distance = plan[n]
-        block = xg.at[x_block(d, distance), parts[half]]
-        return remote(
-            block, block, xg_s.at[n], xg_r.at[n],
-            dev(right if d == 0 else left, z, y, c),
-        )
-
-    for n in (0, 2, 1, 3):
-        x_out(n).start()
+    def x_out(h, n):
+        return x_copy(h, n, plan[n][2] - 1)
+
+    def x_in(h, n):
+        return x_copy(h, n, plan[n][2])
+
+    def x_open(h):
+        for n in (0, 2, 1, 3):
+            x_out(h, n).start()
+
+    def x_forward(h):
+        x_in(h, 0).wait_recv()
+        x_out(h, 4).start()
+        x_in(h, 2).wait_recv()
+        x_out(h, 5).start()
+
+    def x_wait(h):
+        for n in (1, 3, 4, 5):
+            x_in(h, n).wait_recv()
+
+    i = iota((ALL_SLOTS, slots), 0)
+    q = (i * 171) >> 9
+    at = iota((ALL_SLOTS, slots), 1) - (q & (NZ - 1)) * SLOTS - (q >> 4) * 4
+    squeeze = ones_where(at == i - 3 * q)
+    squeeze_spare = ones_where(at == CAP)
+    i = iota((ALL_SLOTS, 128), 0)
+    k_kept = i - 3 * ((i * 171) >> 9)
+    lane = iota((ALL_SLOTS, 128), 1)
+
+    z_wait(0)
+    got = zrecv[0].reshape(slots, SIDE)
+    spare_rows = dot(squeeze_spare, got)
+    first, second = spare_rows[:, 0:128], spare_rows[:, 128:256]
+    tail = jnp.where(
+        k_kept == 0, first, jnp.where(k_kept == 1, pltpu.roll(first, TAIL, 1), second)
+    )
+    flag = jnp.sum(jnp.where(lane == TAIL + k_kept, second, 0.0), axis=1, keepdims=True)
+    tail = jnp.where(lane < TAIL, tail, flag)
+    xg0[x] = jnp.concatenate((dot(squeeze, got), tail), axis=1).astype(BF16)
+    x_open(0)
+    ring_steps(pieces, 2, 3)
+    x_forward(0)
+    z_wait(1)
+    xg1[x] = dot(squeeze, zrecv[1].reshape(slots, SIDE)).astype(BF16)
+    x_open(1)
     ring_steps(pieces, 3, 4)
-    x_in(0).wait_recv()
-    x_out(4).start()
-    x_in(2).wait_recv()
-    x_out(5).start()
-    ring_steps(pieces, 4, 6)
-    for n in (1, 3, 4, 5):
-        x_in(n).wait_recv()
+    x_forward(1)
+    ring_steps(pieces, 4, 5)
+    x_wait(0)
 
     before = ones_where(iota((ALL_SLOTS, ALL_SLOTS), 0) < iota((ALL_SLOTS, ALL_SLOTS), 1))
-    flag_lane = ones_where(iota((16, 128), 1) == FEAT - 512)
+    flag_lane = ones_where(iota((16, 128), 1) == TAIL)
     my_gain = gain[pl.ds(pl.multiple_of(y * NC * FEAT, 128), NC * FEAT)].reshape(1, NC * FEAT)
     my_gain = jnp.where(c == 0, my_gain[:, :FEAT], my_gain[:, FEAT:])
     table = jnp.zeros((8, 128), F32)
@@ -306,18 +357,36 @@
             xs.at[1 - c, dx], xs.at[1 - c, dx], cs_s.at[dx], cs_r.at[dx], dev(x, z, y, 1 - c)
         )
 
+    def keep(dx, low_column, rows):
+        high_column = low_column + rows.shape[1]
+        judged[dx, :, low_column:high_column] = rows.astype(BF16)
+        xs[c, dx, :, low_column:high_column] = (
+            rows * my_gain[:, low_column:high_column]
+        ).astype(BF16)
+        return jnp.sum(rows * rows, axis=1, keepdims=True)
+
+    places, sums = [], []
     for dx in range(NX):
-        s = xg[:, dx * KEPT:(dx + 1) * KEPT, :].reshape(ALL_SLOTS, WIDE)
-        filled = dot(flag_lane, s[:, 512:WIDE], NTR)
+        s = xg0[:, dx * KEPT:(dx + 1) * KEPT, :].reshape(ALL_SLOTS, WIDE)
+        filled = dot(flag_lane, s[:, SIDE:WIDE], NTR)
         rank = dot(filled.astype(BF16), before)
         key = jnp.where(filled > 0.5, rank, -1.0)[0:1]
         place = ones_where(iota((ROWS, ALL_SLOTS), 0).astype(F32) == key)
-        rows = dot(place, s)[:, :FEAT]
-        judged[dx] = rows.astype(BF16)
-        xs[c, dx] = (rows * my_gain).astype(BF16)
+        rows = dot(place, s)
+        places.append(place)
+        sums.append(
+            keep(dx, 0, rows[:, 0:SIDE]) + keep(dx, 2 * SIDE, rows[:, SIDE:SIDE + TAIL])
+        )
+
+    ring_steps(pieces, 5, 6)
+    x_wait(1)
+    for dx in range(NX):
+        s = xg1[:, dx * KEPT:(dx + 1) * KEPT, :].reshape(ALL_SLOTS, SIDE)
+        total = sums[dx] + keep(dx, SIDE, dot(places[dx], s))
         share(dx).start()
-        squares = column_to_row(jnp.sum(rows * rows, axis=1, keepdims=True))
-        table = jnp.where(sub == dx, squares, table)
+        table = jnp.where(sub == dx, column_to_row(total), table)
+        if dx == 1:
+            ring_steps(pieces, 6, last - 1)
 
     sq_in[0] = table
 
@@ -331,7 +400,6 @@
     def _(k):
         squares_out(k).start()
 
-    ring_steps(pieces, 6, last - 1)
     ring_last_sends(pieces)
     ring_close((0, 1))
     for dx in range(NX):
@@ -484,9 +552,10 @@
         turned(True).wait_send()
         turned(False).wait_send()
 
-    @pl.loop(1, NZ)
-    def _(k):
-        z_out(k).wait_send()
+    for h in (0, 1):
+        @pl.loop(1, NZ)
+        def _(k):
+            z_out(h, k).wait_send()
 
     for p in range(3):
         @pl.loop(0, NZ // 2 - 1)
@@ -495,8 +564,9 @@
             ring(p, 1, s, s).wait_send()
 
         ring(p, 0, NZ // 2 - 1, NZ // 2 - 1).wait_send()
-    for n in range(6):
-        x_out(n).wait_send()
+    for h in (0, 1):
+        for n in range(6):
+            x_out(h, n).wait_send()
     for dx in range(NX):
         share(dx).wait_send()
 
@@ -545,15 +615,16 @@
         pltpu.VMEM((WROWS, HD), BF16),
         pltpu.VMEM((WROWS, 256), BF16),
         dma((5,)),
-        pltpu.VMEM((ROWS, WIDE), BF16),
-        pltpu.VMEM((NZ, SLOTS, WIDE), BF16),
-        pltpu.VMEM((NZ, SLOTS, WIDE), BF16),
+        pltpu.VMEM((ROWS, 128), BF16),
+        pltpu.VMEM((2, NZ, SLOTS, SIDE), BF16),
+        pltpu.VMEM((2, NZ, SLOTS, SIDE), BF16),
         pltpu.VMEM((3, 2 * WROWS, HD), BF16),
         pltpu.VMEM((NZ, 3, 2 * WROWS, HD), BF16),
         pltpu.VMEM((3, BLOCK, 2 * HD), F32),
         pltpu.VMEM((8, 128), I32),
         pltpu.VMEM((8, 128), I32),
         pltpu.VMEM((NX, ALL_SLOTS, WIDE), BF16),
+        pltpu.VMEM((NX, ALL_SLOTS, SIDE), BF16),
         pltpu.VMEM((NC, NX, ROWS, FEAT), BF16),
         pltpu.VMEM((NX, ROWS, FEAT), BF16),
         pltpu.VMEM((NT, 8, 128), F32),
@@ -567,9 +638,9 @@
         pltpu.VMEM((NX, ROWS, FEAT), BF16),
         pltpu.VMEM((NX, ROWS, FEAT), BF16),
         dma((2,)), dma((2,)),
-        dma((NZ,)), dma((NZ,)),
+        dma((2, NZ)), dma((2, NZ)),
         dma((3, 2, NZ // 2)), dma((3, 2, NZ // 2)),
-        dma((6,)), dma((6,)),
+        dma((2, 6)), dma((2, 6)),
         dma((NX,)), dma((NX,)),
         dma((NT,)), dma((NT,)),
         dma((NY,)), dma((NY,)),

time: 91 us -> 88.9 us (0.977)
  Pallas kernels: 89.2 us -> 87.2 us
    pallas_call x1, Pallas kernels: 89.2 us -> 87.2 us  [shards(): pl.pallas_call(kernel, out_shape=jax.ShapeDtypeStruct((ROWS, FEAT), BF16)...]
where the time goes in v5:
time: 88.9 us; the launch traced here: 88.7 us
  Pallas kernels  87.2 us (98%)
  local copies, waits for them, and re-layouts  1.56 us (2%)
    pallas_call x1, Pallas kernels, shards(): pl.pallas_call(kernel, out_shape=jax.ShapeDtypeStruct((ROWS, FEAT), BF16)...  87.2 us

profile of v5, /device:TPU:1, one launch (start us, length us, event | category | flops | bytes accessed | tf_op | source)
XLA Modules:
  0.0 88.7 jit_solution(14537931307816132040)
XLA Ops:
  0.0 87.2 %shard_map.100 = bf16[96,576]{1,0:T(8,128)(2,1)} custom-call(bf16[96,576]{1,0:T(8,128)(2,1)} %roll_h.1, s32[1,64]{1,0:T(1,128)} %counts.1, s32[192]{0:T(256)} %lens.1, s32[1,3]{1,0:T(1,128)} %pslot.1, f32[4608]{0:T(1024)} %gain.1, f32[576]{0:T(1024)} %post.1, bf16[72,256]{1,0:T(8,128)(2,1)} %wq_h.1, bf16[72,128]{1,0:T(8,128)(2,1)} %wk_h.1, ...), custom_call_target="tpu_custom_call" | custom-call | tf_op jit(solution)/shard_map/pallas_call | solution.py:653
  87.2 1.6 %copy.12 = bf16[96,576]{1,0:T(8,128)(2,1)} copy(bf16[96,576]{1,0:T(8,128)(2,1)} %shard_map.100) | data formatting | bytes 221184

commit v6 on v5

--- a/solution.py
+++ b/solution.py
@@ -62,9 +62,9 @@
 def kernel(
     roll_h, counts, lens, pslot, gain, post, wq_h, wk_h, wv_h, wo_h, out,
     roll, wq, wk, wv, wo, in_s, low, zsend, zrecv, wsend, wbuf, w32, slot_out, slot_in, xg0, xg1, xs, judged, sq_in, fin_in,
-    part, part_in, far_in, ctx, co_out, co_in, xo_out, xo_in,
+    part, part_in, ctx, co_out, co_in, xo_out, xo_in,
     tr_s, tr_r, za_s, za_r, ring_s, ring_r, xg_s, xg_r, cs_s, cs_r, sq_s, sq_r,
-    rs_s, rs_r, far_s, far_r, cx_s, cx_r, co_s, co_r, xo_s, xo_r, fn_s, fn_r,
+    rs_s, rs_r, cx_s, cx_r, co_s, co_r, xo_s, xo_r, fn_s, fn_r,
 ):
     pair = lax.axis_index("pair")
     ten = lax.axis_index("tensor")
@@ -184,15 +184,14 @@
             zsend.at[h, f], zrecv.at[h, f], za_s.at[h, k], za_r.at[h, k], dev(x, f, y, c)
         )
 
-    def turned(first):
-        if first:
-            return remote(wsend, wbuf.at[z], tr_s.at[0], tr_r.at[0], dev(y, z, x, c))
-        return remote(slot_out, slot_in, tr_s.at[1], tr_r.at[1], dev(y, z, x, c))
+    def turned(p):
+        src, dst = (slot_out, slot_in) if p == 3 else (wsend.at[p], wbuf.at[z, p])
+        return remote(src, dst, tr_s.at[p], tr_r.at[p], dev(y, z, x, c))
 
     @pl.when(off_diagonal)
     def _():
-        turned(True).start()
-        turned(False).start()
+        for p in range(4):
+            turned(p).start()
 
     for h in (0, 1):
         z_out(h, NZ // 2).start()
@@ -224,11 +223,6 @@
         at = pl.ds(pl.multiple_of(block * WROWS, 8), WROWS)
         w32[p, at, 0:HD] = v[:WROWS]
         w32[p, at, HD:2 * HD] = v[WROWS:]
-
-    def ring_open(p):
-        ring(p, 0, 0, 0).start()
-        ring(p, 1, 0, 0).start()
-        unpack(p, z)
 
     def ring_steps(pieces, low, high):
         @pl.loop(low, high)
@@ -257,14 +251,21 @@
             ring(p, 0, last - 1, last).wait_recv()
             unpack(p, ring_block(0, last))
 
+    pieces = (0, 1, 2)
+    for p in pieces:
+        @pl.when(off_diagonal)
+        def _():
+            turned(p).wait_recv()
+
+        ring(p, 0, 0, 0).start()
+        ring(p, 1, 0, 0).start()
+    for p in pieces:
+        unpack(p, z)
+
     @pl.when(off_diagonal)
     def _():
-        turned(True).wait_recv()
-        turned(False).wait_recv()
-
-    pieces = (0, 1, 2)
-    for p in pieces:
-        ring_open(p)
+        turned(3).wait_recv()
+
     ring_steps(pieces, 1, 2)
 
     def z_wait(h):
@@ -332,12 +333,12 @@
     x_open(0)
     ring_steps(pieces, 2, 3)
     x_forward(0)
+    ring_steps(pieces, 3, 4)
     z_wait(1)
     xg1[x] = dot(squeeze, zrecv[1].reshape(slots, SIDE)).astype(BF16)
     x_open(1)
-    ring_steps(pieces, 3, 4)
+    ring_steps(pieces, 4, 5)
     x_forward(1)
-    ring_steps(pieces, 4, 5)
     x_wait(0)
 
     before = ones_where(iota((ALL_SLOTS, ALL_SLOTS), 0) < iota((ALL_SLOTS, ALL_SLOTS), 1))
@@ -377,8 +378,10 @@
         sums.append(
             keep(dx, 0, rows[:, 0:SIDE]) + keep(dx, 2 * SIDE, rows[:, SIDE:SIDE + TAIL])
         )
-
-    ring_steps(pieces, 5, 6)
+        if dx == 1:
+            ring_steps(pieces, 5, 6)
+
+    ring_steps(pieces, 6, last - 1)
     x_wait(1)
     for dx in range(NX):
         s = xg1[:, dx * KEPT:(dx + 1) * KEPT, :].reshape(ALL_SLOTS, SIDE)
@@ -386,7 +389,7 @@
         share(dx).start()
         table = jnp.where(sub == dx, column_to_row(total), table)
         if dx == 1:
-            ring_steps(pieces, 6, last - 1)
+            ring_last_sends(pieces)
 
     sq_in[0] = table
 
@@ -400,32 +403,31 @@
     def _(k):
         squares_out(k).start()
 
-    ring_last_sends(pieces)
     ring_close((0, 1))
     for dx in range(NX):
         share_in(dx).wait_recv()
 
     first = xs[0].reshape(NX * ROWS, FEAT)
     second = xs[1].reshape(NX * ROWS, FEAT)
-    for p in (0, 1):
+    def products(p):
         w = w32[p].astype(BF16)
         t = dot(first, w[:FEAT]) + dot(second, w[FEAT:])
-        part[:, :, p * 256:(p + 1) * 256] = t.astype(BF16).reshape(NX, ROWS, 256)
-
-    def sum_out(k):
+        return t.astype(BF16).reshape(NX, ROWS, 256)
+
+    def sum_out(n, k):
         t = (y + k) % NY
-        return remote(part.at[t], part_in.at[k], rs_s.at[k], rs_r.at[k], dev(x, z, t, c))
-
-    def far_out(k):
-        t = (y + k) % NY
-        return remote(
-            part.at[(t + NY // 2) % NY, :, pl.ds(256, 256)], far_in.at[k],
-            far_s.at[k], far_r.at[k], dev(x, z, t, c),
-        )
-
+        src = (part.at[1, t], part.at[1, (t + NY // 2) % NY], part.at[0, t])[n]
+        return remote(
+            src, part_in.at[n, k], rs_s.at[n, k], rs_r.at[n, k], dev(x, z, t, c)
+        )
+
+    part[1] = products(1)
     for k in (2, 1, 3):
-        sum_out(k).start()
-        far_out(k).start()
+        for n in (0, 1):
+            sum_out(n, k).start()
+    part[0] = products(0)
+    for k in (2, 1, 3):
+        sum_out(2, k).start()
 
     ring_close((2,))
 
@@ -444,14 +446,15 @@
         return lax.rsqrt(row_to_column(row, ROWS) / width + epsilon)
 
     scale_own, scale_far = row_scale(y), row_scale(far_y)
+    for n in range(3):
+        for k in range(1, NY):
+            sum_out(n, k).wait_recv()
+    kv, far, q_own = part[1, y].astype(F32), part[1, far_y].astype(F32), part[0, y].astype(F32)
     for k in range(1, NY):
-        sum_out(k).wait_recv()
-        far_out(k).wait_recv()
-    own = part[y].astype(F32)
-    far = part[far_y, :, 256:512].astype(F32)
-    for k in range(1, NY):
-        own = own + part_in[k].astype(F32)
-        far = far + far_in[k].astype(F32)
+        kv = kv + part_in[0, k].astype(F32)
+        far = far + part_in[1, k].astype(F32)
+        q_own = q_own + part_in[2, k].astype(F32)
+    own = jnp.concatenate((q_own, kv), axis=1)
     own = (own * scale_own).astype(BF16)
     far = (far * scale_far).astype(BF16)
 
@@ -549,8 +552,8 @@
 
     @pl.when(off_diagonal)
     def _():
-        turned(True).wait_send()
-        turned(False).wait_send()
+        for p in range(4):
+            turned(p).wait_send()
 
     for h in (0, 1):
         @pl.loop(1, NZ)
@@ -575,8 +578,8 @@
         squares_out(k).wait_send()
 
     for k in range(1, NY):
-        sum_out(k).wait_send()
-        far_out(k).wait_send()
+        for n in range(3):
+            sum_out(n, k).wait_send()
         ctx_out(k).wait_send()
         xsum(k).wait_send()
     for k in order:
@@ -629,22 +632,20 @@
         pltpu.VMEM((NX, ROWS, FEAT), BF16),
         pltpu.VMEM((NT, 8, 128), F32),
         pltpu.VMEM((NT, 8, 128), F32),
-        pltpu.VMEM((NX, ROWS, 512), BF16),
-        pltpu.VMEM((NY, ROWS, 512), BF16),
-        pltpu.VMEM((NY, ROWS, 256), BF16),
+        pltpu.VMEM((2, NX, ROWS, 256), BF16),
+        pltpu.VMEM((3, NY, ROWS, 256), BF16),
         pltpu.VMEM((NY, ROWS, 256), BF16),
         pltpu.VMEM((NX, ROWS, FEAT), BF16),
         pltpu.VMEM((NX, ROWS, FEAT), BF16),
         pltpu.VMEM((NX, ROWS, FEAT), BF16),
         pltpu.VMEM((NX, ROWS, FEAT), BF16),
-        dma((2,)), dma((2,)),
+        dma((4,)), dma((4,)),
         dma((2, NZ)), dma((2, NZ)),
         dma((3, 2, NZ // 2)), dma((3, 2, NZ // 2)),
         dma((2, 6)), dma((2, 6)),
         dma((NX,)), dma((NX,)),
         dma((NT,)), dma((NT,)),
-        dma((NY,)), dma((NY,)),
-        dma((NY,)), dma((NY,)),
+        dma((3, NY)), dma((3, NY)),
         dma((NY,)), dma((NY,)),
         dma((NX,)), dma((NX,)),
         dma((NX,)), dma((NX,)),

time: 88.9 us -> 88.7 us (level)
  no operation moved by 1% of the time
where the time goes in v6:
time: 88.7 us; the launch traced here: 88.5 us
  Pallas kernels  86.9 us (98%)
  local copies, waits for them, and re-layouts  1.56 us (2%)
    pallas_call x1, Pallas kernels, shards(): pl.pallas_call(kernel, out_shape=jax.ShapeDtypeStruct((ROWS, FEAT), BF16)...  86.9 us

profile of v6, /device:TPU:1, one launch (start us, length us, event | category | flops | bytes accessed | tf_op | source)
XLA Modules:
  0.0 88.5 jit_solution(7347504209840881816)
XLA Ops:
  0.0 86.9 %shard_map.100 = bf16[96,576]{1,0:T(8,128)(2,1)} custom-call(bf16[96,576]{1,0:T(8,128)(2,1)} %roll_h.1, s32[1,64]{1,0:T(1,128)} %counts.1, s32[192]{0:T(256)} %lens.1, s32[1,3]{1,0:T(1,128)} %pslot.1, f32[4608]{0:T(1024)} %gain.1, f32[576]{0:T(1024)} %post.1, bf16[72,256]{1,0:T(8,128)(2,1)} %wq_h.1, bf16[72,128]{1,0:T(8,128)(2,1)} %wk_h.1, ...), custom_call_target="tpu_custom_call" | custom-call | tf_op jit(solution)/shard_map/pallas_call | solution.py:654
  86.9 1.6 %copy.12 = bf16[96,576]{1,0:T(8,128)(2,1)} copy(bf16[96,576]{1,0:T(8,128)(2,1)} %shard_map.100) | data formatting | bytes 221184

commit v7 on v6

--- a/solution.py
+++ b/solution.py
@@ -68,8 +68,8 @@
 ):
     pair = lax.axis_index("pair")
     ten = lax.axis_index("tensor")
-    x, z = pair // NZ, pair % NZ
-    y, c = ten // NC, ten % NC
+    x, z = pair >> 4, pair & (NZ - 1)
+    y, c = ten >> 1, ten & (NC - 1)
 
     def dev(xx, zz, yy, cc):
         return {"pair": xx * NZ + zz, "tensor": yy * NC + cc}
@@ -98,15 +98,15 @@
 
     @pl.loop(1, NZ)
     def _(k):
-        greet(dev(x, (z + k) % NZ, y, c))
+        greet(dev(x, ((z + k) & (NZ - 1)), y, c))
 
     @pl.loop(1, NX)
     def _(k):
-        greet(dev((x + k) % NX, z, y, c))
+        greet(dev(((x + k) & (NX - 1)), z, y, c))
 
     @pl.loop(1, NT)
     def _(k):
-        greet({"pair": pair, "tensor": (ten + k) % NT})
+        greet({"pair": pair, "tensor": ((ten + k) & (NT - 1))})
 
     @pl.when(off_diagonal)
     def _():
@@ -173,13 +173,13 @@
         pl.semaphore_wait(barrier, greeted)
 
     def z_out(h, k):
-        t = (z + k) % NZ
+        t = ((z + k) & (NZ - 1))
         return remote(
             zsend.at[h, t], zrecv.at[h, z], za_s.at[h, k], za_r.at[h, k], dev(x, t, y, c)
         )
 
     def z_in(h, k):
-        f = (z + NZ - k) % NZ
+        f = ((z + NZ - k) & (NZ - 1))
         return remote(
             zsend.at[h, f], zrecv.at[h, f], za_s.at[h, k], za_r.at[h, k], dev(x, f, y, c)
         )
@@ -206,10 +206,10 @@
         wbuf[z] = wsend[...]
         slot_in[...] = slot_out[...]
 
-    up, down = (z + 1) % NZ, (z + NZ - 1) % NZ
+    up, down = ((z + 1) & (NZ - 1)), ((z + NZ - 1) & (NZ - 1))
 
     def ring_block(d, s):
-        return (z + NZ - s) % NZ if d == 0 else (z + s) % NZ
+        return ((z + NZ - s) & (NZ - 1)) if d == 0 else ((z + s) & (NZ - 1))
 
     def ring(p, d, s, distance):
         block = wbuf.at[ring_block(d, distance), p]
@@ -273,7 +273,7 @@
         def _(k):
             z_in(h, k).wait_recv()
 
-    right, left = (x + 1) % NX, (x + NX - 1) % NX
+    right, left = ((x + 1) & (NX - 1)), ((x + NX - 1) & (NX - 1))
     parts = (pl.ds(0, HALF), pl.ds(HALF, HALF))
     plan = (
         (0, 0, 1), (0, 1, 1), (1, 1, 1), (1, 0, 1), (0, 0, 2), (1, 1, 2),
@@ -281,7 +281,7 @@
     held = (xg0, xg1)
 
     def x_block(d, distance):
-        return (x + NX - distance) % NX if d == 0 else (x + distance) % NX
+        return ((x + NX - distance) & (NX - 1)) if d == 0 else ((x + distance) & (NX - 1))
 
     def x_copy(h, n, distance):
         d, half, _ = plan[n]
@@ -396,7 +396,7 @@
     def squares_out(k):
         return remote(
             sq_in.at[0], sq_in.at[k], sq_s.at[k], sq_r.at[k],
-            {"pair": pair, "tensor": (ten + k) % NT},
+            {"pair": pair, "tensor": ((ten + k) & (NT - 1))},
         )
 
     @pl.loop(1, NT)
@@ -415,8 +415,8 @@
         return t.astype(BF16).reshape(NX, ROWS, 256)
 
     def sum_out(n, k):
-        t = (y + k) % NY
-        src = (part.at[1, t], part.at[1, (t + NY // 2) % NY], part.at[0, t])[n]
+        t = ((y + k) & (NY - 1))
+        src = (part.at[1, t], part.at[1, ((t + NY // 2) & (NY - 1))], part.at[0, t])[n]
         return remote(
             src, part_in.at[n, k], rs_s.at[n, k], rs_r.at[n, k], dev(x, z, t, c)
         )
@@ -431,6 +431,33 @@
 
     ring_close((2,))
 
+    @pl.when(off_diagonal)
+    def _():
+        for p in range(4):
+            turned(p).wait_send()
+
+    for h in (0, 1):
+        @pl.loop(1, NZ)
+        def _(k):
+            z_out(h, k).wait_send()
+
+    for p in range(3):
+        @pl.loop(0, NZ // 2 - 1)
+        def _(s):
+            ring(p, 0, s, s).wait_send()
+            ring(p, 1, s, s).wait_send()
+
+        ring(p, 0, NZ // 2 - 1, NZ // 2 - 1).wait_send()
+    for h in (0, 1):
+        for n in range(6):
+            x_out(h, n).wait_send()
+    for dx in range(NX):
+        share(dx).wait_send()
+
+    @pl.loop(1, NT)
+    def _(k):
+        squares_out(k).wait_send()
+
     @pl.loop(1, NT)
     def _(k):
         squares_out(k).wait_recv()
@@ -438,7 +465,7 @@
     total = sq_in[0]
     for k in range(1, NT):
         total = total + sq_in[k]
-    far_y = (y + NY // 2) % NY
+    far_y = ((y + NY // 2) & (NY - 1))
     width = float(NT * FEAT)
 
     def row_scale(which):
@@ -491,10 +518,10 @@
     ctx[y] = jnp.concatenate((mixed[:ROWS], mixed[ROWS:]), axis=1)
 
     def ctx_out(k):
-        return remote(ctx.at[y], ctx.at[y], cx_s.at[k], cx_r.at[k], dev(x, z, (y + k) % NY, c))
+        return remote(ctx.at[y], ctx.at[y], cx_s.at[k], cx_r.at[k], dev(x, z, ((y + k) & (NY - 1)), c))
 
     def ctx_in(k):
-        f = (y + NY - k) % NY
+        f = ((y + NY - k) & (NY - 1))
         return remote(ctx.at[f], ctx.at[f], cx_s.at[k], cx_r.at[k], dev(x, z, f, c))
 
     for k in (2, 1, 3):
@@ -506,31 +533,31 @@
     w_other, w_mine = out_rows(1 - c), out_rows(c)
 
     def swap(k):
-        t = (y + NY - k) % NY
+        t = ((y + NY - k) & (NY - 1))
         return remote(
             co_out.at[t], co_in.at[t], co_s.at[k], co_r.at[k], dev(x, z, y, 1 - c)
         )
 
     def xsum(k):
-        t = (x + k) % NX
+        t = ((x + k) & (NX - 1))
         return remote(xo_out.at[t], xo_in.at[k], xo_s.at[k], xo_r.at[k], dev(t, z, y, c))
 
     order = (0, 1, 3, 2)
     for k in order:
-        t = (y + NY - k) % NY
+        t = ((y + NY - k) & (NY - 1))
         if k > 0:
             ctx_in(k).wait_recv()
         co_out[t] = dot(ctx[t], w_other, NTR).astype(BF16)
         swap(k).start()
         xo_out[t] = dot(ctx[t], w_mine, NTR).astype(BF16)
     for k in order:
-        t = (y + NY - k) % NY
+        t = ((y + NY - k) & (NY - 1))
         swap(k).wait_recv()
         xo_out[t] = (xo_out[t].astype(F32) + co_in[t].astype(F32)).astype(BF16)
 
         @pl.when(t != x)
         def _():
-            xsum((t + NX - x) % NX).start()
+            xsum(((t + NX - x) & (NX - 1))).start()
 
     attended = xo_out[x].astype(F32)
     for k in (1, 3, 2):
@@ -543,39 +570,12 @@
     def fin_out(k):
         return remote(
             fin_in.at[0], fin_in.at[k], fn_s.at[k], fn_r.at[k],
-            {"pair": pair, "tensor": (ten + k) % NT},
+            {"pair": pair, "tensor": ((ten + k) & (NT - 1))},
         )
 
     @pl.loop(1, NT)
     def _(k):
         fin_out(k).start()
-
-    @pl.when(off_diagonal)
-    def _():
-        for p in range(4):
-            turned(p).wait_send()
-
-    for h in (0, 1):
-        @pl.loop(1, NZ)
-        def _(k):
-            z_out(h, k).wait_send()
-
-    for p in range(3):
-        @pl.loop(0, NZ // 2 - 1)
-        def _(s):
-            ring(p, 0, s, s).wait_send()
-            ring(p, 1, s, s).wait_send()
-
-        ring(p, 0, NZ // 2 - 1, NZ // 2 - 1).wait_send()
-    for h in (0, 1):
-        for n in range(6):
-            x_out(h, n).wait_send()
-    for dx in range(NX):
-        share(dx).wait_send()
-
-    @pl.loop(1, NT)
-    def _(k):
-        squares_out(k).wait_send()
 
     for k in range(1, NY):
         for n in range(3):

time: 88.7 us -> 88.8 us (level)
  no operation moved by 1% of the time
where the time goes in v7:
time: 88.8 us; the launch traced here: 88.6 us
  Pallas kernels  87 us (98%)
  local copies, waits for them, and re-layouts  1.56 us (2%)
    pallas_call x1, Pallas kernels, shards(): pl.pallas_call(kernel, out_shape=jax.ShapeDtypeStruct((ROWS, FEAT), BF16)...  87 us

profile of v7, /device:TPU:1, one launch (start us, length us, event | category | flops | bytes accessed | tf_op | source)
XLA Modules:
  0.0 88.6 jit_solution(15530922413732746886)
XLA Ops:
  0.0 87.0 %shard_map.100 = bf16[96,576]{1,0:T(8,128)(2,1)} custom-call(bf16[96,576]{1,0:T(8,128)(2,1)} %roll_h.1, s32[1,64]{1,0:T(1,128)} %counts.1, s32[192]{0:T(256)} %lens.1, s32[1,3]{1,0:T(1,128)} %pslot.1, f32[4608]{0:T(1024)} %gain.1, f32[576]{0:T(1024)} %post.1, bf16[72,256]{1,0:T(8,128)(2,1)} %wq_h.1, bf16[72,128]{1,0:T(8,128)(2,1)} %wk_h.1, ...), custom_call_target="tpu_custom_call" | custom-call | tf_op jit(solution)/shard_map/pallas_call | solution.py:654
  87.0 1.6 %copy.12 = bf16[96,576]{1,0:T(8,128)(2,1)} copy(bf16[96,576]{1,0:T(8,128)(2,1)} %shard_map.100) | data formatting | bytes 221184

commit v8 on v7

--- a/solution.py
+++ b/solution.py
@@ -21,7 +21,6 @@
 SLOTS = NX * 4
 KEPT = NZ * CAP
 ALL_SLOTS = NX * KEPT
-HALF = ALL_SLOTS // 2
 
 score_scale = 144.0 ** (-0.5)
 soft_cap = 50.0
@@ -273,43 +272,26 @@
         def _(k):
             z_in(h, k).wait_recv()
 
-    right, left = ((x + 1) & (NX - 1)), ((x + NX - 1) & (NX - 1))
-    parts = (pl.ds(0, HALF), pl.ds(HALF, HALF))
-    plan = (
-        (0, 0, 1), (0, 1, 1), (1, 1, 1), (1, 0, 1), (0, 0, 2), (1, 1, 2),
-    )
     held = (xg0, xg1)
 
-    def x_block(d, distance):
-        return ((x + NX - distance) & (NX - 1)) if d == 0 else ((x + distance) & (NX - 1))
-
-    def x_copy(h, n, distance):
-        d, half, _ = plan[n]
-        block = held[h].at[x_block(d, distance), parts[half]]
-        return remote(
-            block, block, xg_s.at[h, n], xg_r.at[h, n],
-            dev(right if d == 0 else left, z, y, c),
-        )
-
-    def x_out(h, n):
-        return x_copy(h, n, plan[n][2] - 1)
-
-    def x_in(h, n):
-        return x_copy(h, n, plan[n][2])
+    def x_copy(h, k, block, target):
+        ref = held[h].at[block]
+        return remote(ref, ref, xg_s.at[h, k], xg_r.at[h, k], dev(target, z, y, c))
+
+    def x_out(h, k):
+        return x_copy(h, k, x, (x + k) & (NX - 1))
+
+    def x_in(h, k):
+        f = (x + NX - k) & (NX - 1)
+        return x_copy(h, k, f, f)
 
     def x_open(h):
-        for n in (0, 2, 1, 3):
-            x_out(h, n).start()
-
-    def x_forward(h):
-        x_in(h, 0).wait_recv()
-        x_out(h, 4).start()
-        x_in(h, 2).wait_recv()
-        x_out(h, 5).start()
+        for k in (2, 1, 3):
+            x_out(h, k).start()
 
     def x_wait(h):
-        for n in (1, 3, 4, 5):
-            x_in(h, n).wait_recv()
+        for k in (1, 3, 2):
+            x_in(h, k).wait_recv()
 
     i = iota((ALL_SLOTS, slots), 0)
     q = (i * 171) >> 9
@@ -332,13 +314,11 @@
     xg0[x] = jnp.concatenate((dot(squeeze, got), tail), axis=1).astype(BF16)
     x_open(0)
     ring_steps(pieces, 2, 3)
-    x_forward(0)
     ring_steps(pieces, 3, 4)
     z_wait(1)
     xg1[x] = dot(squeeze, zrecv[1].reshape(slots, SIDE)).astype(BF16)
     x_open(1)
     ring_steps(pieces, 4, 5)
-    x_forward(1)
     x_wait(0)
 
     before = ones_where(iota((ALL_SLOTS, ALL_SLOTS), 0) < iota((ALL_SLOTS, ALL_SLOTS), 1))
@@ -423,11 +403,11 @@
 
     part[1] = products(1)
     for k in (2, 1, 3):
-        for n in (0, 1):
+        sum_out(0, k).start()
+    part[0] = products(0)
+    for n in (2, 1):
+        for k in (2, 1, 3):
             sum_out(n, k).start()
-    part[0] = products(0)
-    for k in (2, 1, 3):
-        sum_out(2, k).start()
 
     ring_close((2,))
 
@@ -449,8 +429,8 @@
 
         ring(p, 0, NZ // 2 - 1, NZ // 2 - 1).wait_send()
     for h in (0, 1):
-        for n in range(6):
-            x_out(h, n).wait_send()
+        for k in range(1, NX):
+            x_out(h, k).wait_send()
     for dx in range(NX):
         share(dx).wait_send()
 
@@ -473,19 +453,18 @@
         return lax.rsqrt(row_to_column(row, ROWS) / width + epsilon)
 
     scale_own, scale_far = row_scale(y), row_scale(far_y)
-    for n in range(3):
+    def summed(n, mine, scale):
         for k in range(1, NY):
             sum_out(n, k).wait_recv()
-    kv, far, q_own = part[1, y].astype(F32), part[1, far_y].astype(F32), part[0, y].astype(F32)
-    for k in range(1, NY):
-        kv = kv + part_in[0, k].astype(F32)
-        far = far + part_in[1, k].astype(F32)
-        q_own = q_own + part_in[2, k].astype(F32)
-    own = jnp.concatenate((q_own, kv), axis=1)
-    own = (own * scale_own).astype(BF16)
-    far = (far * scale_far).astype(BF16)
-
-    queries = jnp.concatenate((own[:, 0:HD], own[:, HD:2 * HD]), axis=0)
+        t = mine.astype(F32)
+        for k in range(1, NY):
+            t = t + part_in[n, k].astype(F32)
+        return (t * scale).astype(BF16)
+
+    kv = summed(0, part[1, y], scale_own)
+    q_own = summed(2, part[0, y], scale_own)
+
+    queries = jnp.concatenate((q_own[:, 0:HD], q_own[:, HD:2 * HD]), axis=0)
     col = iota((2 * ROWS, ROWS), 1)
     row = iota((2 * ROWS, ROWS), 0)
     row = jnp.where(row >= ROWS, row - ROWS, row)
@@ -506,11 +485,13 @@
         scores = soft_cap * jnp.tanh(scores / soft_cap)
         return jnp.exp(jnp.where(ok, scores, negative))
 
-    p_own = powers(own[:, 256:384], own_ok)
-    p_far = powers(far[:, 0:HD], far_ok)
-    whole = jnp.sum(p_own, axis=1, keepdims=True) + jnp.sum(p_far, axis=1, keepdims=True)
-    mixed = dot((p_own / whole).astype(BF16), own[:, 384:512])
-    mixed = mixed + dot((p_far / whole).astype(BF16), far[:, HD:2 * HD])
+    def weigh(keys_values, ok):
+        p = powers(keys_values[:, 0:HD], ok)
+        return jnp.sum(p, axis=1, keepdims=True), dot(p.astype(BF16), keys_values[:, HD:2 * HD])
+
+    whole, mixed = weigh(kv, own_ok)
+    far_whole, far_mixed = weigh(summed(1, part[1, far_y], scale_far), far_ok)
+    mixed = (mixed + far_mixed) / (whole + far_whole)
     row = iota((2 * ROWS, HD), 0)
     row = jnp.where(row >= ROWS, row - ROWS, row)
     present = (row & (LEN - 1)) < by_response(row >> 5, own_lens)
@@ -642,7 +623,7 @@
         dma((4,)), dma((4,)),
         dma((2, NZ)), dma((2, NZ)),
         dma((3, 2, NZ // 2)), dma((3, 2, NZ // 2)),
-        dma((2, 6)), dma((2, 6)),
+        dma((2, NX)), dma((2, NX)),
         dma((NX,)), dma((NX,)),
         dma((NT,)), dma((NT,)),
         dma((3, NY)), dma((3, NY)),

time: 88.8 us -> 88.4 us (level)
  no operation moved by 1% of the time
where the time goes in v8:
time: 88.4 us; the launch traced here: 88.2 us
  Pallas kernels  86.6 us (98%)
  local copies, waits for them, and re-layouts  1.56 us (2%)
    pallas_call x1, Pallas kernels, shards(): pl.pallas_call(kernel, out_shape=jax.ShapeDtypeStruct((ROWS, FEAT), BF16)...  86.6 us

profile of v8, /device:TPU:1, one launch (start us, length us, event | category | flops | bytes accessed | tf_op | source)
XLA Modules:
  0.0 88.2 jit_solution(3998659865800612149)
XLA Ops:
  0.0 86.6 %shard_map.100 = bf16[96,576]{1,0:T(8,128)(2,1)} custom-call(bf16[96,576]{1,0:T(8,128)(2,1)} %roll_h.1, s32[1,64]{1,0:T(1,128)} %counts.1, s32[192]{0:T(256)} %lens.1, s32[1,3]{1,0:T(1,128)} %pslot.1, f32[4608]{0:T(1024)} %gain.1, f32[576]{0:T(1024)} %post.1, bf16[72,256]{1,0:T(8,128)(2,1)} %wq_h.1, bf16[72,128]{1,0:T(8,128)(2,1)} %wk_h.1, ...), custom_call_target="tpu_custom_call" | custom-call | tf_op jit(solution)/shard_map/pallas_call | solution.py:635
  86.6 1.6 %copy.12 = bf16[96,576]{1,0:T(8,128)(2,1)} copy(bf16[96,576]{1,0:T(8,128)(2,1)} %shard_map.100) | data formatting | bytes 221184

commit v9 on v8

--- a/solution.py
+++ b/solution.py
@@ -250,22 +250,23 @@
             ring(p, 0, last - 1, last).wait_recv()
             unpack(p, ring_block(0, last))
 
-    pieces = (0, 1, 2)
-    for p in pieces:
+    early, late = (0, 1), (2,)
+    for p in (0, 1, 2):
         @pl.when(off_diagonal)
         def _():
             turned(p).wait_recv()
 
-        ring(p, 0, 0, 0).start()
-        ring(p, 1, 0, 0).start()
-    for p in pieces:
+        if p in early:
+            ring(p, 0, 0, 0).start()
+            ring(p, 1, 0, 0).start()
+    for p in (0, 1, 2):
         unpack(p, z)
 
     @pl.when(off_diagonal)
     def _():
         turned(3).wait_recv()
 
-    ring_steps(pieces, 1, 2)
+    ring_steps(early, 1, 2)
 
     def z_wait(h):
         @pl.loop(1, NZ)
@@ -313,12 +314,15 @@
     tail = jnp.where(lane < TAIL, tail, flag)
     xg0[x] = jnp.concatenate((dot(squeeze, got), tail), axis=1).astype(BF16)
     x_open(0)
-    ring_steps(pieces, 2, 3)
-    ring_steps(pieces, 3, 4)
+    ring_steps(early, 2, 3)
+    for d in (0, 1):
+        ring(2, d, 0, 0).start()
+    ring_steps(early, 3, 4)
     z_wait(1)
     xg1[x] = dot(squeeze, zrecv[1].reshape(slots, SIDE)).astype(BF16)
     x_open(1)
-    ring_steps(pieces, 4, 5)
+    ring_steps(early, 4, 5)
+    ring_steps(late, 1, 2)
     x_wait(0)
 
     before = ones_where(iota((ALL_SLOTS, ALL_SLOTS), 0) < iota((ALL_SLOTS, ALL_SLOTS), 1))
@@ -359,9 +363,11 @@
             keep(dx, 0, rows[:, 0:SIDE]) + keep(dx, 2 * SIDE, rows[:, SIDE:SIDE + TAIL])
         )
         if dx == 1:
-            ring_steps(pieces, 5, 6)
-
-    ring_steps(pieces, 6, last - 1)
+            ring_steps(early, 5, 6)
+            ring_steps(late, 2, 3)
+
+    ring_steps(early, 6, last - 1)
+    ring_steps(late, 3, 4)
     x_wait(1)
     for dx in range(NX):
         s = xg1[:, dx * KEPT:(dx + 1) * KEPT, :].reshape(ALL_SLOTS, SIDE)
@@ -369,7 +375,8 @@
         share(dx).start()
         table = jnp.where(sub == dx, column_to_row(total), table)
         if dx == 1:
-            ring_last_sends(pieces)
+            ring_last_sends(early)
+            ring_steps(late, 4, 5)
 
     sq_in[0] = table
 
@@ -383,7 +390,7 @@
     def _(k):
         squares_out(k).start()
 
-    ring_close((0, 1))
+    ring_close(early)
     for dx in range(NX):
         share_in(dx).wait_recv()
 
@@ -409,7 +416,7 @@
         for k in (2, 1, 3):
             sum_out(n, k).start()
 
-    ring_close((2,))
+    ring_steps(late, 5, last - 1)
 
     @pl.when(off_diagonal)
     def _():
@@ -421,13 +428,16 @@
         def _(k):
             z_out(h, k).wait_send()
 
-    for p in range(3):
-        @pl.loop(0, NZ // 2 - 1)
+    def ring_left(p):
+        @pl.loop(0, last - 1)
         def _(s):
             ring(p, 0, s, s).wait_send()
             ring(p, 1, s, s).wait_send()
 
-        ring(p, 0, NZ // 2 - 1, NZ // 2 - 1).wait_send()
+        ring(p, 0, last - 1, last - 1).wait_send()
+
+    for p in early:
+        ring_left(p)
     for h in (0, 1):
         for k in range(1, NX):
             x_out(h, k).wait_send()
@@ -490,6 +500,7 @@
         return jnp.sum(p, axis=1, keepdims=True), dot(p.astype(BF16), keys_values[:, HD:2 * HD])
 
     whole, mixed = weigh(kv, own_ok)
+    ring_last_sends(late)
     far_whole, far_mixed = weigh(summed(1, part[1, far_y], scale_far), far_ok)
     mixed = (mixed + far_mixed) / (whole + far_whole)
     row = iota((2 * ROWS, HD), 0)
@@ -507,6 +518,7 @@
 
     for k in (2, 1, 3):
         ctx_out(k).start()
+    ring_close(late)
 
     def out_rows(half):
         return w32[2, pl.ds(pl.multiple_of(half * FEAT, 8), FEAT), :].astype(BF16)
@@ -558,6 +570,7 @@
     def _(k):
         fin_out(k).start()
 
+    ring_left(2)
     for k in range(1, NY):
         for n in range(3):
             sum_out(n, k).wait_send()

time: 88.4 us -> 88.6 us (level)
  no operation moved by 1% of the time
where the time goes in v9:
time: 88.6 us; the launch traced here: 88.4 us
  Pallas kernels  86.8 us (98%)
  local copies, waits for them, and re-layouts  1.56 us (2%)
    pallas_call x1, Pallas kernels, shards(): pl.pallas_call(kernel, out_shape=jax.ShapeDtypeStruct((ROWS, FEAT), BF16)...  86.8 us

profile of v9, /device:TPU:1, one launch (start us, length us, event | category | flops | bytes accessed | tf_op | source)
XLA Modules:
  0.0 88.4 jit_solution(8793773896050701921)
XLA Ops:
  0.0 86.8 %shard_map.100 = bf16[96,576]{1,0:T(8,128)(2,1)} custom-call(bf16[96,576]{1,0:T(8,128)(2,1)} %roll_h.1, s32[1,64]{1,0:T(1,128)} %counts.1, s32[192]{0:T(256)} %lens.1, s32[1,3]{1,0:T(1,128)} %pslot.1, f32[4608]{0:T(1024)} %gain.1, f32[576]{0:T(1024)} %post.1, bf16[72,256]{1,0:T(8,128)(2,1)} %wq_h.1, bf16[72,128]{1,0:T(8,128)(2,1)} %wk_h.1, ...), custom_call_target="tpu_custom_call" | custom-call | tf_op jit(solution)/shard_map/pallas_call | solution.py:648
  86.8 1.6 %copy.12 = bf16[96,576]{1,0:T(8,128)(2,1)} copy(bf16[96,576]{1,0:T(8,128)(2,1)} %shard_map.100) | data formatting | bytes 221184

commit v10 on v9

--- a/solution.py
+++ b/solution.py
@@ -208,13 +208,13 @@
     up, down = ((z + 1) & (NZ - 1)), ((z + NZ - 1) & (NZ - 1))
 
     def ring_block(d, s):
-        return ((z + NZ - s) & (NZ - 1)) if d == 0 else ((z + s) & (NZ - 1))
+        return ((z + NZ - s) & (NZ - 1)) if d == 1 else ((z + s) & (NZ - 1))
 
     def ring(p, d, s, distance):
         block = wbuf.at[ring_block(d, distance), p]
         return remote(
             block, block, ring_s.at[p, d, s], ring_r.at[p, d, s],
-            dev(x, up if d == 0 else down, y, c),
+            dev(x, up if d == 1 else down, y, c),
         )
 
     def unpack(p, block):

time: 88.6 us -> 88.8 us (level)
  no operation moved by 1% of the time
where the time goes in v10:
time: 88.8 us; the launch traced here: 88.5 us
  Pallas kernels  87 us (98%)
  local copies, waits for them, and re-layouts  1.56 us (2%)
    pallas_call x1, Pallas kernels, shards(): pl.pallas_call(kernel, out_shape=jax.ShapeDtypeStruct((ROWS, FEAT), BF16)...  87 us

profile of v10, /device:TPU:1, one launch (start us, length us, event | category | flops | bytes accessed | tf_op | source)
XLA Modules:
  0.0 88.5 jit_solution(11404624599651618665)
XLA Ops:
  0.0 87.0 %shard_map.100 = bf16[96,576]{1,0:T(8,128)(2,1)} custom-call(bf16[96,576]{1,0:T(8,128)(2,1)} %roll_h.1, s32[1,64]{1,0:T(1,128)} %counts.1, s32[192]{0:T(256)} %lens.1, s32[1,3]{1,0:T(1,128)} %pslot.1, f32[4608]{0:T(1024)} %gain.1, f32[576]{0:T(1024)} %post.1, bf16[72,256]{1,0:T(8,128)(2,1)} %wq_h.1, bf16[72,128]{1,0:T(8,128)(2,1)} %wk_h.1, ...), custom_call_target="tpu_custom_call" | custom-call | tf_op jit(solution)/shard_map/pallas_call | solution.py:648
  87.0 1.6 %copy.12 = bf16[96,576]{1,0:T(8,128)(2,1)} copy(bf16[96,576]{1,0:T(8,128)(2,1)} %shard_map.100) | data formatting | bytes 221184

commit v11 on v10

--- a/solution.py
+++ b/solution.py
@@ -61,7 +61,7 @@
 def kernel(
     roll_h, counts, lens, pslot, gain, post, wq_h, wk_h, wv_h, wo_h, out,
     roll, wq, wk, wv, wo, in_s, low, zsend, zrecv, wsend, wbuf, w32, slot_out, slot_in, xg0, xg1, xs, judged, sq_in, fin_in,
-    part, part_in, ctx, co_out, co_in, xo_out, xo_in,
+    part, part_in, ycomb, ctx, co_out, co_in, xo_out, xo_in,
     tr_s, tr_r, za_s, za_r, ring_s, ring_r, xg_s, xg_r, cs_s, cs_r, sq_s, sq_r,
     rs_s, rs_r, cx_s, cx_r, co_s, co_r, xo_s, xo_r, fn_s, fn_r,
 ):
@@ -401,20 +401,34 @@
         t = dot(first, w[:FEAT]) + dot(second, w[FEAT:])
         return t.astype(BF16).reshape(NX, ROWS, 256)
 
-    def sum_out(n, k):
-        t = ((y + k) & (NY - 1))
-        src = (part.at[1, t], part.at[1, ((t + NY // 2) & (NY - 1))], part.at[0, t])[n]
-        return remote(
-            src, part_in.at[n, k], rs_s.at[n, k], rs_r.at[n, k], dev(x, z, t, c)
-        )
-
-    part[1] = products(1)
-    for k in (2, 1, 3):
-        sum_out(0, k).start()
-    part[0] = products(0)
-    for n in (2, 1):
-        for k in (2, 1, 3):
-            sum_out(n, k).start()
+    key_values = products(1)
+    part[:, :, 256:512] = key_values
+    for dx in range(NX):
+        part[dx, :, 512:768] = key_values[(dx + NX // 2) % NX]
+    part[:, :, 0:256] = products(0)
+
+    halves = (pl.ds(0, ROWS // 2), pl.ds(ROWS // 2, ROWS // 2))
+
+    def y_near(d):
+        return ((y + 1) & (NY - 1)) if d == 0 else ((y + NY - 1) & (NY - 1))
+
+    def ysum(stage, d):
+        t = y_near(d)
+        src = (
+            part.at[(y + NY // 2) & (NY - 1), halves[d]], part.at[t, halves[1 - d]], ycomb.at[d]
+        )[stage]
+        return remote(
+            src, part_in.at[stage, d], rs_s.at[stage, d], rs_r.at[stage, d], dev(x, z, t, c)
+        )
+
+    for stage in (0, 1):
+        for d in (0, 1):
+            ysum(stage, d).start()
+    for d in (0, 1):
+        ysum(0, d).wait_recv()
+        mine = part[y_near(d), halves[d]].astype(F32)
+        ycomb[d] = (mine + part_in[0, d].astype(F32)).astype(BF16)
+        ysum(2, d).start()
 
     ring_steps(late, 5, last - 1)
 
@@ -463,16 +477,19 @@
         return lax.rsqrt(row_to_column(row, ROWS) / width + epsilon)
 
     scale_own, scale_far = row_scale(y), row_scale(far_y)
-    def summed(n, mine, scale):
-        for k in range(1, NY):
-            sum_out(n, k).wait_recv()
-        t = mine.astype(F32)
-        for k in range(1, NY):
-            t = t + part_in[n, k].astype(F32)
-        return (t * scale).astype(BF16)
-
-    kv = summed(0, part[1, y], scale_own)
-    q_own = summed(2, part[0, y], scale_own)
+    for stage in (1, 2):
+        for d in (0, 1):
+            ysum(stage, d).wait_recv()
+    both = part[y].astype(F32) + jnp.concatenate(
+        (
+            part_in[2, 0].astype(F32) + part_in[1, 1].astype(F32),
+            part_in[2, 1].astype(F32) + part_in[1, 0].astype(F32),
+        ),
+        axis=0,
+    )
+    q_own = (both[:, 0:256] * scale_own).astype(BF16)
+    kv = (both[:, 256:512] * scale_own).astype(BF16)
+    kv_far = (both[:, 512:768] * scale_far).astype(BF16)
 
     queries = jnp.concatenate((q_own[:, 0:HD], q_own[:, HD:2 * HD]), axis=0)
     col = iota((2 * ROWS, ROWS), 1)
@@ -501,7 +518,7 @@
 
     whole, mixed = weigh(kv, own_ok)
     ring_last_sends(late)
-    far_whole, far_mixed = weigh(summed(1, part[1, far_y], scale_far), far_ok)
+    far_whole, far_mixed = weigh(kv_far, far_ok)
     mixed = (mixed + far_mixed) / (whole + far_whole)
     row = iota((2 * ROWS, HD), 0)
     row = jnp.where(row >= ROWS, row - ROWS, row)
@@ -570,10 +587,11 @@
     def _(k):
         fin_out(k).start()
 
+    for stage in range(3):
+        for d in (0, 1):
+            ysum(stage, d).wait_send()
     ring_left(2)
     for k in range(1, NY):
-        for n in range(3):
-            sum_out(n, k).wait_send()
         ctx_out(k).wait_send()
         xsum(k).wait_send()
     for k in order:
@@ -626,8 +644,9 @@
         pltpu.VMEM((NX, ROWS, FEAT), BF16),
         pltpu.VMEM((NT, 8, 128), F32),
         pltpu.VMEM((NT, 8, 128), F32),
-        pltpu.VMEM((2, NX, ROWS, 256), BF16),
-        pltpu.VMEM((3, NY, ROWS, 256), BF16),
+        pltpu.VMEM((NX, ROWS, 768), BF16),
+        pltpu.VMEM((3, 2, ROWS // 2, 768), BF16),
+        pltpu.VMEM((2, ROWS // 2, 768), BF16),
         pltpu.VMEM((NY, ROWS, 256), BF16),
         pltpu.VMEM((NX, ROWS, FEAT), BF16),
         pltpu.VMEM((NX, ROWS, FEAT), BF16),
@@ -639,7 +658,7 @@
         dma((2, NX)), dma((2, NX)),
         dma((NX,)), dma((NX,)),
         dma((NT,)), dma((NT,)),
-        dma((3, NY)), dma((3, NY)),
+        dma((3, 2)), dma((3, 2)),
         dma((NY,)), dma((NY,)),
         dma((NX,)), dma((NX,)),
         dma((NX,)), dma((NX,)),

time: 88.8 us -> 91.7 us (1.033)
  Pallas kernels: 87 us -> 89.9 us
    pallas_call x1, Pallas kernels: 87 us -> 89.9 us  [shards(): pl.pallas_call(kernel, out_shape=jax.ShapeDtypeStruct((ROWS, FEAT), BF16)...]
where the time goes in v11:
time: 91.7 us; the launch traced here: 91.5 us
  Pallas kernels  89.9 us (98%)
  local copies, waits for them, and re-layouts  1.56 us (2%)
    pallas_call x1, Pallas kernels, shards(): pl.pallas_call(kernel, out_shape=jax.ShapeDtypeStruct((ROWS, FEAT), BF16)...  89.9 us

profile of v11, /device:TPU:1, one launch (start us, length us, event | category | flops | bytes accessed | tf_op | source)
XLA Modules:
  0.0 91.5 jit_solution(356241367843430593)
XLA Ops:
  0.0 89.9 %shard_map.100 = bf16[96,576]{1,0:T(8,128)(2,1)} custom-call(bf16[96,576]{1,0:T(8,128)(2,1)} %roll_h.1, s32[1,64]{1,0:T(1,128)} %counts.1, s32[192]{0:T(256)} %lens.1, s32[1,3]{1,0:T(1,128)} %pslot.1, f32[4608]{0:T(1024)} %gain.1, f32[576]{0:T(1024)} %post.1, bf16[72,256]{1,0:T(8,128)(2,1)} %wq_h.1, bf16[72,128]{1,0:T(8,128)(2,1)} %wk_h.1, ...), custom_call_target="tpu_custom_call" | custom-call | tf_op jit(solution)/shard_map/pallas_call | solution.py:667
  89.9 1.6 %copy.12 = bf16[96,576]{1,0:T(8,128)(2,1)} copy(bf16[96,576]{1,0:T(8,128)(2,1)} %shard_map.100) | data formatting | bytes 221184

commit v12 on v10

--- a/solution.py
+++ b/solution.py
@@ -315,14 +315,13 @@
     xg0[x] = jnp.concatenate((dot(squeeze, got), tail), axis=1).astype(BF16)
     x_open(0)
     ring_steps(early, 2, 3)
-    for d in (0, 1):
-        ring(2, d, 0, 0).start()
     ring_steps(early, 3, 4)
     z_wait(1)
     xg1[x] = dot(squeeze, zrecv[1].reshape(slots, SIDE)).astype(BF16)
     x_open(1)
     ring_steps(early, 4, 5)
-    ring_steps(late, 1, 2)
+    for d in (0, 1):
+        ring(2, d, 0, 0).start()
     x_wait(0)
 
     before = ones_where(iota((ALL_SLOTS, ALL_SLOTS), 0) < iota((ALL_SLOTS, ALL_SLOTS), 1))
@@ -364,10 +363,10 @@
         )
         if dx == 1:
             ring_steps(early, 5, 6)
-            ring_steps(late, 2, 3)
+            ring_steps(late, 1, 2)
 
     ring_steps(early, 6, last - 1)
-    ring_steps(late, 3, 4)
+    ring_steps(late, 2, 3)
     x_wait(1)
     for dx in range(NX):
         s = xg1[:, dx * KEPT:(dx + 1) * KEPT, :].reshape(ALL_SLOTS, SIDE)
@@ -376,7 +375,7 @@
         table = jnp.where(sub == dx, column_to_row(total), table)
         if dx == 1:
             ring_last_sends(early)
-            ring_steps(late, 4, 5)
+            ring_steps(late, 3, 4)
 
     sq_in[0] = table
 
@@ -416,7 +415,7 @@
         for k in (2, 1, 3):
             sum_out(n, k).start()
 
-    ring_steps(late, 5, last - 1)
+    ring_steps(late, 4, last - 1)
 
     @pl.when(off_diagonal)
     def _():

time: 88.8 us -> 91.5 us (1.030)
  Pallas kernels: 87 us -> 89.7 us
    pallas_call x1, Pallas kernels: 87 us -> 89.7 us  [shards(): pl.pallas_call(kernel, out_shape=jax.ShapeDtypeStruct((ROWS, FEAT), BF16)...]
where the time goes in v12:
time: 91.5 us; the launch traced here: 91.2 us
  Pallas kernels  89.7 us (98%)
  local copies, waits for them, and re-layouts  1.56 us (2%)
    pallas_call x1, Pallas kernels, shards(): pl.pallas_call(kernel, out_shape=jax.ShapeDtypeStruct((ROWS, FEAT), BF16)...  89.7 us

profile of v12, /device:TPU:1, one launch (start us, length us, event | category | flops | bytes accessed | tf_op | source)
XLA Modules:
  0.0 91.2 jit_solution(7591020814264951863)
XLA Ops:
  0.0 89.7 %shard_map.100 = bf16[96,576]{1,0:T(8,128)(2,1)} custom-call(bf16[96,576]{1,0:T(8,128)(2,1)} %roll_h.1, s32[1,64]{1,0:T(1,128)} %counts.1, s32[192]{0:T(256)} %lens.1, s32[1,3]{1,0:T(1,128)} %pslot.1, f32[4608]{0:T(1024)} %gain.1, f32[576]{0:T(1024)} %post.1, bf16[72,256]{1,0:T(8,128)(2,1)} %wq_h.1, bf16[72,128]{1,0:T(8,128)(2,1)} %wk_h.1, ...), custom_call_target="tpu_custom_call" | custom-call | tf_op jit(solution)/shard_map/pallas_call | solution.py:647
  89.7 1.6 %copy.12 = bf16[96,576]{1,0:T(8,128)(2,1)} copy(bf16[96,576]{1,0:T(8,128)(2,1)} %shard_map.100) | data formatting | bytes 221184

commit v13 on v12

--- a/solution.py
+++ b/solution.py
@@ -267,6 +267,8 @@
         turned(3).wait_recv()
 
     ring_steps(early, 1, 2)
+    for d in (0, 1):
+        ring(2, d, 0, 0).start()
 
     def z_wait(h):
         @pl.loop(1, NZ)
@@ -316,12 +318,12 @@
     x_open(0)
     ring_steps(early, 2, 3)
     ring_steps(early, 3, 4)
+    ring_steps(late, 1, 2)
     z_wait(1)
     xg1[x] = dot(squeeze, zrecv[1].reshape(slots, SIDE)).astype(BF16)
     x_open(1)
     ring_steps(early, 4, 5)
-    for d in (0, 1):
-        ring(2, d, 0, 0).start()
+    ring_steps(late, 2, 3)
     x_wait(0)
 
     before = ones_where(iota((ALL_SLOTS, ALL_SLOTS), 0) < iota((ALL_SLOTS, ALL_SLOTS), 1))
@@ -363,10 +365,10 @@
         )
         if dx == 1:
             ring_steps(early, 5, 6)
-            ring_steps(late, 1, 2)
+            ring_steps(late, 3, 4)
 
     ring_steps(early, 6, last - 1)
-    ring_steps(late, 2, 3)
+    ring_steps(late, 4, 5)
     x_wait(1)
     for dx in range(NX):
         s = xg1[:, dx * KEPT:(dx + 1) * KEPT, :].reshape(ALL_SLOTS, SIDE)
@@ -375,7 +377,7 @@
         table = jnp.where(sub == dx, column_to_row(total), table)
         if dx == 1:
             ring_last_sends(early)
-            ring_steps(late, 3, 4)
+            ring_steps(late, 5, 6)
 
     sq_in[0] = table
 
@@ -415,7 +417,7 @@
         for k in (2, 1, 3):
             sum_out(n, k).start()
 
-    ring_steps(late, 4, last - 1)
+    ring_steps(late, 6, last - 1)
 
     @pl.when(off_diagonal)
     def _():

time: 91.5 us -> 88.7 us (0.969)
  Pallas kernels: 89.7 us -> 86.9 us
    pallas_call x1, Pallas kernels: 89.7 us -> 86.9 us  [shards(): pl.pallas_call(kernel, out_shape=jax.ShapeDtypeStruct((ROWS, FEAT), BF16)...]
where the time goes in v13:
time: 88.7 us; the launch traced here: 88.5 us
  Pallas kernels  86.9 us (98%)
  local copies, waits for them, and re-layouts  1.56 us (2%)
    pallas_call x1, Pallas kernels, shards(): pl.pallas_call(kernel, out_shape=jax.ShapeDtypeStruct((ROWS, FEAT), BF16)...  86.9 us

profile of v13, /device:TPU:1, one launch (start us, length us, event | category | flops | bytes accessed | tf_op | source)
XLA Modules:
  0.0 88.5 jit_solution(13609001606650460682)
XLA Ops:
  0.0 86.9 %shard_map.100 = bf16[96,576]{1,0:T(8,128)(2,1)} custom-call(bf16[96,576]{1,0:T(8,128)(2,1)} %roll_h.1, s32[1,64]{1,0:T(1,128)} %counts.1, s32[192]{0:T(256)} %lens.1, s32[1,3]{1,0:T(1,128)} %pslot.1, f32[4608]{0:T(1024)} %gain.1, f32[576]{0:T(1024)} %post.1, bf16[72,256]{1,0:T(8,128)(2,1)} %wq_h.1, bf16[72,128]{1,0:T(8,128)(2,1)} %wk_h.1, ...), custom_call_target="tpu_custom_call" | custom-call | tf_op jit(solution)/shard_map/pallas_call | solution.py:649
  86.9 1.6 %copy.12 = bf16[96,576]{1,0:T(8,128)(2,1)} copy(bf16[96,576]{1,0:T(8,128)(2,1)} %shard_map.100) | data formatting | bytes 221184
